TPU v7x, 32 devices: a whole 2x2x4 slice. The times are simulated.
32 devices in a mesh: store: 8 (over z, core), own: 4 (over y, x).
Axes of the slice: x: 2, y: 2, z: 4, core: 2. Of those that a mesh axis runs over, the one named last changes fastest.
Arguments:
- embed: bfloat16 [8192, 768], P(('store', 'own')), may hold values from -16 to 16
- cluster: int32 [8192], P(('store', 'own')), may hold values from 0 to 511, as said below
- rank: int32 [8192], P(('store', 'own')), may hold values from 0 to 8191, each once
Outputs:
- best_similarity: float32 [8192], P(('store', 'own'))
Inputs may be any that keep to these rules, and one draw needn't show every extreme that they name: Among the 256 rows of one device, at most 33 have clusters with one owner (cluster mod 8); every device reaches 33 for some owners, and some owner gets exactly 33 from every device. `rank`: every value appears once.
All inputs are finite; a program needn't handle non-finite values.
Results may differ from a plain program's by a relative error of at most 0.00064.
Values may be sent and summed in bfloat16 or wider, within the bound.
No kernel may reach another device: no remote copies, remote signals or barrier semaphores. Data moves between devices by JAX's collectives and lax.ppermute only.
A program may use at most 64 MiB of HBM per device.

v0:
```python
import jax
import jax.numpy as jnp
from jax import lax
from jax.sharding import PartitionSpec as P


def pair_maxima(left_rows, left_cluster, left_rank, right_rows, right_cluster, right_rank):
    scores = jnp.einsum("qd,kd->qk", left_rows, right_rows, preferred_element_type=jnp.float32)
    usable = (
        (left_cluster[:, None] == right_cluster[None, :])
        & (right_rank[None, :] < left_rank[:, None])
        & (left_cluster[:, None] >= 0)
    )
    return jnp.max(jnp.where(usable, scores, -1.0), axis=1)


def local(embed, cluster, rank):
    row_count = embed.shape[0]
    store_size = lax.axis_size("store")
    capacity = row_count // store_size + 1
    slot_count = store_size * capacity
    widened = embed.astype(jnp.float32)
    unit_rows = (
        widened * lax.rsqrt(jnp.sum(widened * widened, axis=1, keepdims=True) + 1e-06)
    ).astype(jnp.bfloat16)
    target = cluster % store_size
    onehot = (target[:, None] == jnp.arange(store_size, dtype=jnp.int32)[None, :]).astype(jnp.int32)
    before = jnp.cumsum(onehot, axis=0) - onehot
    within = jnp.sum(before * onehot, axis=1)
    position = target * capacity + within
    placed = jnp.arange(slot_count, dtype=jnp.int32)[:, None] == position[None, :]
    outgoing = jnp.dot(
        placed.astype(jnp.bfloat16), unit_rows, preferred_element_type=jnp.float32
    ).astype(jnp.bfloat16)
    out_cluster = jnp.sum(jnp.where(placed, cluster[None, :] + 1, 0), axis=1) - 1
    out_rank = jnp.sum(jnp.where(placed, rank[None, :], 0), axis=1)
    queries, query_cluster, query_rank = (
        lax.all_to_all(outgoing, "store", split_axis=0, concat_axis=0, tiled=True),
        lax.all_to_all(out_cluster, "store", split_axis=0, concat_axis=0, tiled=True),
        lax.all_to_all(out_rank, "store", split_axis=0, concat_axis=0, tiled=True),
    )
    start_best = jnp.full((slot_count,), -1.0, jnp.float32)
    best_match = jnp.maximum(
        start_best,
        pair_maxima(
            queries,
            query_cluster,
            query_rank,
            lax.all_gather(queries, "own", axis=0, tiled=True),
            lax.all_gather(query_cluster, "own", axis=0, tiled=True),
            lax.all_gather(query_rank, "own", axis=0, tiled=True),
        ),
    )
    returned = lax.all_to_all(best_match, "store", split_axis=0, concat_axis=0, tiled=True)
    return jnp.sum(jnp.where(placed, returned[:, None], 0.0), axis=0)


def solution(mesh):
    return jax.shard_map(
        local,
        mesh=mesh,
        in_specs=(P(("store", "own"), None), P(("store", "own")), P(("store", "own"))),
        out_specs=P(("store", "own")),
        check_vma=False,
    )
```

profile of v0, /device:TPU:0, one launch (start us, length us, event | category | flops | bytes accessed | tf_op | source)
XLA Modules:
  0.0 87.8 jit_solution(3690726193899705804)
XLA Ops:
  6.5 0.7 broadcast_add_fusion.1
  7.2 0.6 reduce-window.6
  8.2 1.2 %fusion.1 = f32[256]{0:T(256)S(1)} fusion(bf16[256,768]{1,0:T(8,128)(2,1)} %param.3), kind=kLoop, calls=%fused_computation.5 | loop fusion | flops 589568 | bytes 394240 | tf_op jit(solution)/shard_map/reduce_sum | solution.py:24
  9.3 1.4 %convolution_convert_fusion = bf16[264,768]{1,0:T(8,128)(2,1)S(1)} fusion(bf16[256,768]{1,0:T(8,128)(2,1)} %param.3, f32[256]{0:T(256)S(1)} %add_rsqrt_fusion, s32[256]{0:T(256)S(1)} %multiply_add_fusion), kind=kOutput, calls=%fused_computation.2 | convolution fusion | flops 104669184 | bytes 800768 | tf_op jit(solution)/shard_map/dot_general | solution.py:32
  10.9 20.8 %all_to_all.36 = bf16[8,33,768]{2,1,0:T(8,128)(2,1)S(1)} all-to-all(bf16[8,33,768]{2,1,0:T(8,128)(2,1)S(1)} %all_to_all.28), channel_id=1, replica_groups=mesh['store'=8,'own'=4] {'store'}, dimensions={0} | all-to-all | bytes 811008 | tf_op jit(solution)/shard_map/all_to_all | solution.py:38
  31.7 0.9 %all_to_all.30 = bf16[264,768]{1,0:T(8,128)(2,1)} reshape(bf16[8,33,768]{2,1,0:T(8,128)(2,1)S(1)} %all_to_all.36) | data formatting | bytes 811008 | tf_op jit(solution)/shard_map/all_to_all | solution.py:38
  32.8 0.7 sub.11
  33.5 3.2 %all-to-all-start = ((s32[8,33,1]{1,2,0:T(1,128)}), s32[8,33,1]{1,2,0:T(1,128)S(1)}, u32[]{:S(2)}, u32[]{:S(2)}) async-start(s32[8,33,1]{1,2,0:T(1,128)} %bitcast.3), calls=%async_computation | async-start | bytes 8192 | tf_op jit(solution)/shard_map/all_to_all | solution.py:39
  36.7 0.7 all_to_all.25
  37.4 4.8 %all-to-all-done = s32[8,33,1]{1,2,0:T(1,128)S(1)} async-done(((s32[8,33,1]{1,2,0:T(1,128)}), s32[8,33,1]{1,2,0:T(1,128)S(1)}, u32[]{:S(2)}, u32[]{:S(2)}) %all-to-all-start) | async-done | bytes 1088 | tf_op jit(solution)/shard_map/all_to_all | solution.py:39
  42.2 3.3 %all-to-all-start.1 = ((s32[8,33,1]{1,2,0:T(1,128)}), s32[8,33,1]{1,2,0:T(1,128)S(1)}, u32[]{:S(2)}, u32[]{:S(2)}) async-start(s32[8,33,1]{1,2,0:T(1,128)} %bitcast.5), calls=%async_computation.1 | async-start | bytes 8192 | tf_op jit(solution)/shard_map/all_to_all | solution.py:40
  45.5 0.6 dynamic-slice
  46.8 0.5 broadcast.78
  47.3 0.7 reduce.12
  48.0 3.0 %all-to-all-done.1 = s32[8,33,1]{1,2,0:T(1,128)S(1)} async-done(((s32[8,33,1]{1,2,0:T(1,128)}), s32[8,33,1]{1,2,0:T(1,128)S(1)}, u32[]{:S(2)}, u32[]{:S(2)}) %all-to-all-start.1) | async-done | bytes 1088 | tf_op jit(solution)/shard_map/all_to_all | solution.py:40
  51.0 0.7 reduce.11
  51.7 0.3 dynamic-update-slice
  52.0 0.3 dynamic-update-slice.1
  52.3 16.2 %all-reduce.2 = (s32[1056]{0:T(1024)S(1)}, s32[1056]{0:T(1024)S(1)}) all-reduce(s32[1056]{0:T(1024)S(1)} %dynamic-update-slice.1, s32[1056]{0:T(1024)S(1)} %dynamic-update-slice), channel_id=1, replica_groups=mesh['store'=8,'own'=4] {'own'}, use_global_device_ids=true, to_apply=%add.1 | all-reduce | flops 2112 | bytes 16896
  68.6 2.4 %fusion = f32[264]{0:T(512)S(1)} fusion(bf16[264,768]{1,0:T(8,128)(2,1)} %all_to_all.30, bf16[1056,768]{1,0:T(8,128)(2,1)} %all-gather.2.cloned.1.call-done, s32[1056]{0:T(1024)S(1)} %get-tuple-element.7, s32[1056]{0:T(1024)S(1)} %get-tuple-element.8, s32[264]{0:T(512)S(1)} %reshape.76, s32[264]{0:T(512)S(1)} %reshape.73, ...), kind=kOutput, calls=%fused_computation.1 | convolution fusion | flops 429884672 | bytes 2039400 | tf_op jit(solution)/shard_map/qd,kd->qk/dot_general | solution.py:8
  71.1 7.9 %all_to_all.37 = f32[8,33,1]{1,2,0:T(1,128)S(1)} all-to-all(f32[8,33,1]{1,2,0:T(1,128)S(1)} %bitcast.18), channel_id=1, replica_groups=mesh['store'=8,'own'=4] {'store'}, dimensions={0} | all-to-all | bytes 2112 | tf_op jit(solution)/shard_map/all_to_all | solution.py:54
  79.0 0.5 broadcast.80
  79.5 0.7 reduce.13
  80.2 0.7 select_reduce_fusion
  (25 shorter events, 1.1 us)
Async XLA Ops:
  6.5 62.0 %all-gather.2.cloned.1.call-start = ((), (), s32[]{:S(2)}) async-start(), calls=%async_computation.4 | async-start | bytes 2027520 | tf_op jit(solution)/shard_map/all_gather | solution.py:49
  10.9 21.7 %copy-start = (s32[256]{0:T(256)S(1)}, s32[256]{0:T(256)}, u32[]{:S(2)}) copy-start(s32[256]{0:T(256)} %param.5) | copy-start | bytes 3076
  10.9 34.6 %copy-start.1 = (u32[32]{0:T(128)S(1)}, u32[32]{0:T(128)}, u32[]{:S(2)}) copy-start(u32[32]{0:T(128)} %constant.39) | copy-start | bytes 388
  33.5 8.7 %all-to-all-start = ((s32[8,33,1]{1,2,0:T(1,128)}), s32[8,33,1]{1,2,0:T(1,128)S(1)}, u32[]{:S(2)}, u32[]{:S(2)}) async-start(s32[8,33,1]{1,2,0:T(1,128)} %bitcast.3), calls=%async_computation | async-start | bytes 8192 | tf_op jit(solution)/shard_map/all_to_all | solution.py:39
  42.2 8.8 %all-to-all-start.1 = ((s32[8,33,1]{1,2,0:T(1,128)}), s32[8,33,1]{1,2,0:T(1,128)S(1)}, u32[]{:S(2)}, u32[]{:S(2)}) async-start(s32[8,33,1]{1,2,0:T(1,128)} %bitcast.5), calls=%async_computation.1 | async-start | bytes 8192 | tf_op jit(solution)/shard_map/all_to_all | solution.py:40
Sparse Core Ops, SparseCore 0:
  32.7 30.6 all-gather.1
where the time goes:
time: 88.2 us; the launch traced here: 87.8 us
  blocking collectives  45 us (51%)
  between operations  14.2 us (16%)
  waiting for transfers between devices  7.83 us (9%)
  starting transfers between devices  6.54 us (7%)
  other arithmetic  5.44 us (6%)
  local copies, waits for them, and re-layouts  5.07 us (6%)
  matrix products  3.77 us (4%)
    all_to_all x1, blocking collectives, local(): lax.all_to_all(outgoing, 'store', split_axis=0, concat_axis=0, tiled=True)  20.8 us
    unnamed x1, blocking collectives  16.2 us
    all_to_all x1, blocking collectives, local(): lax.all_to_all(best_match, 'store', split_axis=0, concat_axis=0, tiled=True)  7.92 us
    all_to_all x1, waiting for transfers between devices, local(): lax.all_to_all(out_cluster, 'store', split_axis=0, concat_axis=0, tiled=T...  4.82 us
    all_to_all x1, starting transfers between devices, local(): lax.all_to_all(out_rank, 'store', split_axis=0, concat_axis=0, tiled=True)  3.31 us
    all_to_all x1, starting transfers between devices, local(): lax.all_to_all(out_cluster, 'store', split_axis=0, concat_axis=0, tiled=T...  3.22 us
    all_to_all x1, waiting for transfers between devices, local(): lax.all_to_all(out_rank, 'store', split_axis=0, concat_axis=0, tiled=True)  2.97 us
    dot_general x1, matrix products, pair_maxima(): jnp.einsum('qd,kd->qk', left_rows, right_rows, preferred_element_type=jnp...  2.41 us
  transfers between devices with their start and end apart: 3, of which 2 were waited for; matrix products, arithmetic and copies ran while one was open for 5% of the time, Pallas kernels for 0%

commit v1 on v0

v1 whole, which is shorter than its diff:
```python
import functools
from typing import NamedTuple

import jax
import jax.numpy as jnp
from jax import lax
from jax.experimental import pallas as pl
from jax.experimental.pallas import tpu as pltpu
from jax.sharding import Mesh, PartitionSpec as P

LANES = 128
TAIL = 16
CLUSTER_DIGITS = 2
RANK_DIGITS = 3
VMEM_LIMIT = 48 * 1024 * 1024


class Shape(NamedTuple):
    rows: int
    width: int
    z: int
    x: int
    y: int

    @property
    def classes(self):
        return self.z * self.x

    @property
    def capacity(self):
        return self.rows // self.classes + 1

    @property
    def base(self):
        return max(16, (self.rows // self.classes) // 16 * 16)

    @property
    def extra(self):
        return max(0, self.capacity - self.base)

    @property
    def stride(self):
        return self.base + 8 * self.extra

    @property
    def chunks(self):
        return self.width // LANES

    @property
    def tail_at(self):
        return self.chunks * self.base

    @property
    def block_rows(self):
        return self.tail_at + TAIL

    @property
    def per_lane_tile(self):
        return LANES // self.base

    @property
    def query_rows(self):
        return self.classes * self.base + (-(-self.classes // 16) * 16 if self.extra else 0)


def iota(shape, dim):
    return lax.broadcasted_iota(jnp.int32, shape, dim)


def my_class(s):
    return lax.axis_index("z") * s.x + lax.axis_index("x")


def row_of(ref):
    return jnp.concatenate([ref[i : i + 1, :] for i in range(ref.shape[0])], axis=1)


def dot(left, right, contract=((1,), (0,))):
    return lax.dot_general(left, right, (contract, ((), ())), preferred_element_type=jnp.float32)


def place_kernel(s, layout, embed_ref, cluster_ref, rank_ref, info_ref, *out_refs):
    widened = embed_ref[...].astype(jnp.float32)
    total = jnp.sum(widened * widened, axis=1, keepdims=True)
    unit = (widened * lax.rsqrt(total + 1e-06)).astype(jnp.bfloat16)
    cluster = row_of(cluster_ref)
    rank = row_of(rank_ref)
    n = s.classes
    shift = n.bit_length() - 1
    target = cluster & (n - 1)
    relative = target ^ my_class(s)
    member = (iota((n, s.rows), 0) == relative).astype(jnp.float32)
    earlier = (iota((s.rows, s.rows), 0) < iota((s.rows, s.rows), 1)).astype(jnp.float32)
    before = dot(member.astype(jnp.bfloat16), earlier.astype(jnp.bfloat16))
    within = jnp.sum(before * member, axis=0, keepdims=True).astype(jnp.int32)
    position = relative * s.stride + within
    placed = (iota((n * s.stride, s.rows), 0) == position).astype(jnp.float32).astype(jnp.bfloat16)
    grouped = dot(placed, unit)
    local = (cluster >> shift) + 1
    digits = [(local >> (8 * i)) & 255 for i in range(CLUSTER_DIGITS)]
    digits += [(rank >> (8 * i)) & 255 for i in range(RANK_DIGITS)]
    line = iota((TAIL, s.rows), 0)
    fields = jnp.zeros((TAIL, s.rows), jnp.int32)
    for i, digit in enumerate(digits):
        fields = jnp.where(line == s.chunks + i, digit, fields)
    spread = dot(fields.astype(jnp.float32).astype(jnp.bfloat16), placed, ((1,), (1,)))
    tail_line = iota((TAIL, LANES), 0)
    for ref, members in zip(out_refs, layout):
        for slot, r in enumerate(members):
            at = r * s.stride
            for c in range(s.chunks):
                ref[slot, c * s.base : (c + 1) * s.base, :] = grouped[
                    at : at + s.base, c * LANES : (c + 1) * LANES
                ].astype(jnp.bfloat16)
            tail = jnp.concatenate(
                [spread[:, at : at + s.stride], jnp.zeros((TAIL, LANES - s.stride), jnp.float32)], axis=1
            )
            if s.extra:
                for c in range(s.chunks):
                    piece = grouped[at + s.base : at + s.base + 1, c * LANES : (c + 1) * LANES]
                    tail = jnp.where(tail_line == c, piece, tail)
            ref[slot, s.tail_at : s.block_rows, :] = tail.astype(jnp.bfloat16)
    info_ref[...] = jnp.concatenate([target, within], axis=0)


def place(s, layout, embed, cluster, rank):
    outs = [jax.ShapeDtypeStruct((2, s.rows), jnp.int32)]
    outs += [jax.ShapeDtypeStruct((len(m), s.block_rows, LANES), jnp.bfloat16) for m in layout]
    return pl.pallas_call(
        functools.partial(place_kernel, s, layout),
        out_shape=outs,
        compiler_params=pltpu.CompilerParams(vmem_limit_bytes=VMEM_LIMIT),
        name="place",
    )(embed, cluster.reshape(-1, LANES), rank.reshape(-1, LANES))


def blocks_of(refs):
    return [(ref, j) for ref in refs for j in range(ref.shape[0])]


def unpack(s, blocks, rows_ref, tail_ref):
    for b, (ref, j) in enumerate(blocks):
        for c in range(s.chunks):
            rows_ref[b * s.base : (b + 1) * s.base, c * LANES : (c + 1) * LANES] = ref[
                j, c * s.base : (c + 1) * s.base, :
            ]
        tail_ref[b * TAIL : (b + 1) * TAIL, :] = ref[j, s.tail_at : s.block_rows, :]


def sorted_tails(s, tails, blocks, group):
    per = blocks // group
    padded = -(-per // 8) * 8
    used = s.chunks + CLUSTER_DIGITS + RANK_DIGITS
    lines = used * group * padded
    line = iota((lines, blocks * TAIL), 0)
    r = line % padded
    rest = line // padded
    m = rest % group
    field = rest // group
    source = jnp.where(r < per, (r * group + m) * TAIL + field, -1)
    pick = (iota((lines, blocks * TAIL), 1) == source).astype(jnp.float32).astype(jnp.bfloat16)
    picked = dot(pick, tails)
    step = group * padded
    parts = [picked[f * step : (f + 1) * step] for f in range(used)]
    at = s.chunks
    cluster = parts[at] + 256.0 * parts[at + 1]
    at += CLUSTER_DIGITS
    rank = parts[at] + 256.0 * parts[at + 1] + 65536.0 * parts[at + 2]
    return parts[: s.chunks], cluster, rank, padded


def key_lines(s, field, padded, group):
    lane = iota((padded, LANES), 1)
    result = jnp.zeros((padded, LANES), jnp.float32)
    for m in range(group):
        part = jnp.where(lane < s.base, field[m * padded : (m + 1) * padded], 0.0)
        result = result + (pltpu.roll(part, m * s.base, 1) if m else part)
    return result


def load_queries(s, blocks, rows_ref, tail_ref, query_cluster_ref, query_rank_ref):
    n = len(blocks)
    unpack(s, blocks, rows_ref, tail_ref)
    pieces, cluster, rank, _ = sorted_tails(s, tail_ref[: n * TAIL, :], n, 1)
    for field, ref in ((cluster, query_cluster_ref), (rank, query_rank_ref)):
        columns = field.T
        for b in range(n):
            ref[b * s.base : (b + 1) * s.base, :] = jnp.broadcast_to(
                columns[: s.base, b : b + 1], (s.base, LANES)
            )
        if s.extra:
            at = n * s.base
            ref[at : at + n, :] = jnp.broadcast_to(field[:n, s.base : s.base + 1], (n, LANES))
            if s.query_rows > at + n:
                ref[at + n :, :] = jnp.zeros((s.query_rows - at - n, LANES), jnp.float32)
    if s.extra:
        at = n * s.base
        for c, piece in enumerate(pieces):
            spare = s.query_rows - at - piece.shape[0]
            if spare:
                piece = jnp.concatenate([piece, jnp.zeros((spare, LANES), jnp.float32)], axis=0)
            rows_ref[at:, c * LANES : (c + 1) * LANES] = piece.astype(jnp.bfloat16)


def match_keys(s, blocks, keys_ref, tail_ref, queries_ref, query_cluster_ref, query_rank_ref, best):
    n = len(blocks)
    group = s.per_lane_tile
    unpack(s, blocks, keys_ref, tail_ref)
    pieces, cluster, rank, padded = sorted_tails(s, tail_ref[: n * TAIL, :], n, group)
    key_cluster = key_lines(s, cluster, padded, group)
    key_rank = key_lines(s, rank, padded, group)
    queries = queries_ref[...]
    query_cluster = query_cluster_ref[...]
    query_rank = query_rank_ref[...]

    def take(best, scores, line_cluster, line_rank):
        usable = (query_cluster == line_cluster) & (line_rank < query_rank)
        return jnp.maximum(best, jnp.where(usable, scores, -1.0))

    tiles = n // group
    for first in range(0, tiles, 2):
        count = min(2, tiles - first)
        keys = keys_ref[first * LANES : (first + count) * LANES, :]
        scores = dot(queries, keys, ((1,), (1,)))
        for i in range(count):
            t = first + i
            best = take(
                best, scores[:, i * LANES : (i + 1) * LANES], key_cluster[t : t + 1], key_rank[t : t + 1]
            )
    if s.extra:
        count = group * padded
        spare = LANES - count
        for c, piece in enumerate(pieces):
            padded_piece = jnp.concatenate([piece, jnp.zeros((spare, LANES), jnp.float32)], axis=0) if spare else piece
            keys_ref[tiles * LANES :, c * LANES : (c + 1) * LANES] = padded_piece.astype(jnp.bfloat16)
        scores = dot(queries, keys_ref[tiles * LANES :, :], ((1,), (1,)))
        lines = []
        for field in (cluster, rank):
            line = field.T[s.base : s.base + 1, :]
            lines.append(jnp.concatenate([line, jnp.zeros((1, spare), jnp.float32)], axis=1) if spare else line)
        best = take(best, scores, *lines)
    return best


def write_best(s, order, best, out_ref):
    n = s.classes
    column = jnp.max(best, axis=1, keepdims=True)
    eye = iota((s.base, LANES), 0) == iota((s.base, LANES), 1)
    lane = iota((1, LANES), 1)
    me = my_class(s)
    for b, r in enumerate(order):
        line = jnp.sum(jnp.where(eye, column[b * s.base : (b + 1) * s.base], 0.0), axis=0, keepdims=True)
        if s.extra:
            at = n * s.base + b
            line = jnp.where(lane == s.base, column[at : at + 1], line)
        out_ref[pl.ds(me ^ r, 1), :, :] = line[None]


def first_kernel(s, order, query_count, key_count, last, *refs):
    refs = list(refs)
    query_blocks = blocks_of(refs[:query_count])
    key_refs = refs[query_count : query_count + key_count]
    outs = refs[query_count + key_count :]
    queries_ref, query_cluster_ref, query_rank_ref, best_ref, query_tail, keys_ref, key_tail = outs
    load_queries(s, query_blocks, queries_ref, query_tail, query_cluster_ref, query_rank_ref)
    best = jnp.full((s.query_rows, LANES), -1.0, jnp.float32)
    best = match_keys(
        s, query_blocks + blocks_of(key_refs), keys_ref, key_tail, queries_ref, query_cluster_ref, query_rank_ref, best
    )
    if last:
        write_best(s, order, best, best_ref)
    else:
        best_ref[...] = best


def next_kernel(s, order, key_count, last, *refs):
    queries_ref, query_cluster_ref, query_rank_ref, best_ref = refs[:4]
    key_refs = refs[4 : 4 + key_count]
    out_ref, keys_ref, key_tail = refs[4 + key_count :]
    best = match_keys(
        s, blocks_of(key_refs), keys_ref, key_tail, queries_ref, query_cluster_ref, query_rank_ref, best_ref[...]
    )
    if last:
        write_best(s, order, best, out_ref)
    else:
        out_ref[...] = best


def key_scratch(s, blocks):
    rows = blocks * s.base + (LANES if s.extra else 0)
    return [pltpu.VMEM((rows, s.width), jnp.bfloat16), pltpu.VMEM((blocks * TAIL, LANES), jnp.bfloat16)]


def cost(s, blocks):
    keys = blocks * s.base
    return pl.CostEstimate(
        flops=2 * s.query_rows * keys * s.width,
        transcendentals=0,
        bytes_accessed=2 * blocks * s.block_rows * LANES,
    )


def match_first(s, order, queries, keys, last):
    blocks = sum(a.shape[0] for a in queries + keys)
    best_shape = (s.classes, 1, LANES) if last else (s.query_rows, LANES)
    return pl.pallas_call(
        functools.partial(first_kernel, s, order, len(queries), len(keys), last),
        out_shape=[
            jax.ShapeDtypeStruct((s.query_rows, s.width), jnp.bfloat16),
            jax.ShapeDtypeStruct((s.query_rows, LANES), jnp.float32),
            jax.ShapeDtypeStruct((s.query_rows, LANES), jnp.float32),
            jax.ShapeDtypeStruct(best_shape, jnp.float32),
        ],
        scratch_shapes=[pltpu.VMEM((s.classes * TAIL, LANES), jnp.bfloat16)] + key_scratch(s, blocks),
        compiler_params=pltpu.CompilerParams(vmem_limit_bytes=VMEM_LIMIT),
        cost_estimate=cost(s, blocks),
        name="match_first",
    )(*queries, *keys)


def match_next(s, order, state, keys, last):
    blocks = sum(a.shape[0] for a in keys)
    best_shape = (s.classes, 1, LANES) if last else (s.query_rows, LANES)
    best = pl.pallas_call(
        functools.partial(next_kernel, s, order, len(keys), last),
        out_shape=jax.ShapeDtypeStruct(best_shape, jnp.float32),
        scratch_shapes=key_scratch(s, blocks),
        compiler_params=pltpu.CompilerParams(vmem_limit_bytes=VMEM_LIMIT),
        cost_estimate=cost(s, blocks),
        name="match_next",
    )(*state, *keys)
    return [*state[:3], best]


def collect_kernel(s, info_ref, best_ref, out_ref):
    n = s.classes
    best = best_ref[...].reshape(n, LANES)
    parts = []
    for _ in range(3):
        part = best.astype(jnp.bfloat16)
        parts.append(part.astype(jnp.float32))
        best = best - parts[-1]
    target = info_ref[0:1, :]
    within = info_ref[1:2, :]
    pick = (iota((LANES, s.rows), 0) == within).astype(jnp.float32).astype(jnp.bfloat16)
    found = dot(jnp.concatenate(parts, axis=0).astype(jnp.bfloat16), pick)
    found = found[:n] + found[n : 2 * n] + found[2 * n :]
    mine = iota((n, s.rows), 0) == target
    line = jnp.sum(jnp.where(mine, found, 0.0), axis=0, keepdims=True)
    for i in range(s.rows // LANES):
        out_ref[i : i + 1, :] = line[:, i * LANES : (i + 1) * LANES]


def collect(s, info, best):
    out = pl.pallas_call(
        functools.partial(collect_kernel, s),
        out_shape=jax.ShapeDtypeStruct((s.rows // LANES, LANES), jnp.float32),
        name="collect",
    )(info, best)
    return out.reshape(s.rows)


def swap(array, axis, flip):
    size = lax.axis_size(axis)
    return lax.ppermute(array, axis, [(i, i ^ flip) for i in range(size)])


def local(embed, cluster, rank):
    s = Shape(embed.shape[0], embed.shape[1], lax.axis_size("z"), lax.axis_size("x"), lax.axis_size("y"))
    own = [[s.x * k] for k in range(s.z)]
    far = [s.x * k + 1 for k in range(s.z // 2, s.z)]
    near = [s.x * k + 1 for k in range(s.z // 2)]
    info, *arrays = place(s, own + [far, near], embed, cluster, rank)
    owned, (far_rows, near_rows) = arrays[: s.z], arrays[s.z :]
    crossed = jnp.concatenate([swap(near_rows, "x", 1), swap(far_rows, "x", 1)])
    arrived = [
        jnp.concatenate([owned[k], crossed[k : k + 1]]) for k in range(s.z)
    ]
    arrived = [swap(a, "z", k) if k else a for k, a in enumerate(arrived)]
    order = [s.x * k + j for k in range(s.z) for j in range(s.x)]
    if s.y == 2:
        waves = []
        for a in arrived:
            over = swap(a, "y", 1)
            waves.append([swap(a, "core", 1), over, swap(over, "core", 1)])
        state = match_first(s, order, arrived, [], False)
        for i, keys in enumerate(waves):
            if i % 2 == 1:
                state = match_next(s, order, state, waves[i - 1] + keys, i == len(waves) - 1)
    else:
        both = jnp.concatenate(arrived)
        everyone = lax.all_gather(both, ("core", "y"), axis=0)
        state = match_first(s, order, [both], [], False)
        me = lax.axis_index(("core", "y"))
        size = everyone.shape[0]
        for i in range(1, size):
            keys = lax.dynamic_index_in_dim(everyone, (me + i) % size, keepdims=False)
            state = match_next(s, order, state, [keys], i == size - 1)
    returned = lax.all_to_all(state[3], ("z", "x"), split_axis=0, concat_axis=0, tiled=True)
    return collect(s, info, returned)


def solution(mesh):
    store, own = mesh.shape["store"], mesh.shape["own"]
    split = Mesh(mesh.devices.reshape(store // 2, 2, own // 2, 2), ("z", "core", "y", "x"))
    spread = ("z", "core", "y", "x")
    return jax.shard_map(
        local,
        mesh=split,
        in_specs=(P(spread, None), P(spread), P(spread)),
        out_specs=P(spread),
        check_vma=False,
    )
```

time: 88.2 us -> 44.5 us (0.50)
  blocking collectives: 45 us -> 11.9 us
  between operations: 14.2 us -> 0.12 us
  starting transfers between devices: 6.54 us -> 13.5 us
  other arithmetic: 5.44 us -> 0.05 us
  waiting for transfers between devices: 7.83 us -> 13.2 us
  Pallas kernels: 0 us -> 3.82 us
  matrix products: 3.77 us -> 0 us
  local copies, waits for them, and re-layouts: 5.07 us -> 1.71 us
    all_to_all x2 -> x1, blocking collectives: 28.7 us -> 11.9 us  [local(): lax.all_to_all(state[3], ('z', 'x'), split_axis=0, concat_axis=0, tiled=T...]
    unnamed x1 -> x0, blocking collectives: 16.2 us -> none
    ppermute x0 -> x17, starting transfers between devices: none -> 13.5 us  [swap(): return lax.ppermute(array, axis, [(i, i ^ flip) for i in range(size)])]
    ppermute x0 -> x17, waiting for transfers between devices: none -> 13.2 us  [swap(): return lax.ppermute(array, axis, [(i, i ^ flip) for i in range(size)])]
    all_to_all x2 -> x0, waiting for transfers between devices: 7.79 us -> none  [the longest x1 4.82 us: local(): lax.all_to_all(out_cluster, 'store', split_axis=0, concat_axis=0, tiled=T...]
    all_to_all x2 -> x0, starting transfers between devices: 6.54 us -> none  [the longest x1 3.31 us: local(): lax.all_to_all(out_rank, 'store', split_axis=0, concat_axis=0, tiled=True)]
    pallas_call x0 -> x5, Pallas kernels: none -> 3.82 us  [the longest x1 1.4 us: collect(): pl.pallas_call(functools.partial(collect_kernel, s), out_shape=jax.ShapeD...]
    dot_general x2 -> x0, matrix products: 3.77 us -> none  [the longest x1 2.41 us: pair_maxima(): jnp.einsum('qd,kd->qk', left_rows, right_rows, preferred_element_type=jnp...]
  transfers between devices with their start and end apart: 3 -> 17, of which waited for: 2 -> 7; matrix products, arithmetic and copies ran while one was open for 5% -> 0% of each run, Pallas kernels for 0% -> 3%
where the time goes in v1:
time: 44.5 us; the launch traced here: 44.3 us
  starting transfers between devices  13.5 us (30%)
  waiting for transfers between devices  13.2 us (30%)
  blocking collectives  11.9 us (27%)
  Pallas kernels  3.82 us (9%)
  local copies, waits for them, and re-layouts  1.71 us (4%)
    ppermute x17, starting transfers between devices, swap(): return lax.ppermute(array, axis, [(i, i ^ flip) for i in range(size)])  13.5 us
    ppermute x17, waiting for transfers between devices, swap(): return lax.ppermute(array, axis, [(i, i ^ flip) for i in range(size)])  13.2 us
    all_to_all x1, blocking collectives, local(): lax.all_to_all(state[3], ('z', 'x'), split_axis=0, concat_axis=0, tiled=T...  11.9 us
    unnamed x8, local copies, waits for them, and re-layouts  1.69 us
    pallas_call x1, Pallas kernels, collect(): pl.pallas_call(functools.partial(collect_kernel, s), out_shape=jax.ShapeD...  1.4 us
    pallas_call x2, Pallas kernels, match_next(): pl.pallas_call(functools.partial(next_kernel, s, order, len(keys), last),...  1.32 us
  transfers between devices with their start and end apart: 17, of which 7 were waited for; matrix products, arithmetic and copies ran while one was open for 0% of the time, Pallas kernels for 3%

profile of v1, /device:TPU:0, one launch (start us, length us, event | category | flops | bytes accessed | tf_op | source)
XLA Modules:
  0.0 44.3 jit_solution(2434434501958719289)
XLA Ops:
  0.0 0.7 %copy-done.3 = s32[256]{0:T(256)S(1)} copy-done((s32[256]{0:T(256)S(1)}, s32[256]{0:T(256)}, u32[]{:S(2)}) %copy-start.3) | copy-done | bytes 1048
  0.7 1.0 %copy-done = bf16[256,768]{1,0:T(8,128)(2,1)S(1)} copy-done((bf16[256,768]{1,0:T(8,128)(2,1)S(1)}, bf16[256,768]{1,0:T(8,128)(2,1)}, u32[]{:S(2)}) %copy-start) | copy-done | bytes 393240
  1.7 0.5 %place.1 = (s32[2,256]{1,0:T(2,128)S(1)}, bf16[1,208,128]{2,1,0:T(8,128)(2,1)S(1)}, bf16[1,208,128]{2,1,0:T(8,128)(2,1)S(1)}, bf16[1,208,128]{2,1,0:T(8,128)(2,1...) custom-call(bf16[256,768]{1,0:T(8,128)(2,1)S(1)} %copy-done, ...), custom_call_target="tpu_custom_call" | custom-call | tf_op jit(solution)/shard_map/place/pallas_call | solution.py:129
  2.2 3.0 %collective-permute-start = (bf16[2,208,128]{2,1,0:T(8,128)(2,1)S(1)}, bf16[2,208,128]{2,1,0:T(8,128)(2,1)S(1)}, u32[]{:S(2)}, u32[]{:S(2)}) collective-permute-start(bf16[2,208,128]{2,1,0:T(8,128)(2,1)S(1)} %get-tuple-element.18), channel_id=1, source_target_pairs={{0,1},{1,0},{2,3},{3,2},{4,5},{5,4},{6,7},{7,6},{8,9},{9,8},{10,11... | collective-permute-start | bytes 319496 | tf_op jit(solution)/shard_map/ppermute | solution.py:365
  5.2 0.1 collective-permute-start.2
  5.3 3.7 %collective-permute-done = bf16[2,208,128]{2,1,0:T(8,128)(2,1)S(1)} collective-permute-done((bf16[2,208,128]{2,1,0:T(8,128)(2,1)S(1)}, bf16[2,208,128]{2,1,0:T(8,128)(2,1)S(1)}, u32[]{:S(2)}, u32[]{:S(2)}) %collective-permute-start) | collective-permute-done | bytes 106528 | tf_op jit(solution)/shard_map/ppermute | solution.py:365
  9.1 2.1 %collective-permute-start.1 = (bf16[2,208,128]{2,1,0:T(8,128)(2,1)S(1)}, bf16[2,208,128]{2,1,0:T(8,128)(2,1)S(1)}, u32[]{:S(2)}, u32[]{:S(2)}) collective-permute-start(bf16[2,208,128]{2,1,0:T(8,128)(2,1)S(1)} %pad_maximum_fusion.1), channel_id=1, source_target_pairs={{0,8},{8,0},{16,24},{24,16},{1,9},{9,1},{17,25},{25,17},{2,10},{10... | collective-permute-start | bytes 319496 | tf_op jit(solution)/shard_map/ppermute | solution.py:365
  11.2 2.7 %collective-permute-start.3 = (bf16[2,208,128]{2,1,0:T(8,128)(2,1)S(1)}, bf16[2,208,128]{2,1,0:T(8,128)(2,1)S(1)}, u32[]{:S(2)}, u32[]{:S(2)}) collective-permute-start(bf16[2,208,128]{2,1,0:T(8,128)(2,1)S(1)} %pad_maximum_fusion.2), channel_id=1, source_target_pairs={{0,16},{8,24},{16,0},{24,8},{1,17},{9,25},{17,1},{25,9},{2,18},{10... | collective-permute-start | bytes 319496 | tf_op jit(solution)/shard_map/ppermute | solution.py:365
  13.9 1.6 %collective-permute-start.6 = (bf16[2,208,128]{2,1,0:T(8,128)(2,1)S(1)}, bf16[2,208,128]{2,1,0:T(8,128)(2,1)S(1)}, u32[]{:S(2)}, u32[]{:S(2)}) collective-permute-start(bf16[2,208,128]{2,1,0:T(8,128)(2,1)S(1)} %pad_maximum_fusion.refs_0_), channel_id=1, source_target_pairs={{0,2},{2,0},{1,3},{3,1},{4,6},{6,4},{5,7},{7,5},{8,10},{10,8},{9,1... | collective-permute-start | bytes 319496 | tf_op jit(solution)/shard_map/ppermute | solution.py:365
  15.5 0.9 %collective-permute-start.4 = (bf16[2,208,128]{2,1,0:T(8,128)(2,1)S(1)}, bf16[2,208,128]{2,1,0:T(8,128)(2,1)S(1)}, u32[]{:S(2)}, u32[]{:S(2)}) collective-permute-start(bf16[2,208,128]{2,1,0:T(8,128)(2,1)S(1)} %pad_maximum_fusion.3), channel_id=1, source_target_pairs={{0,24},{8,16},{16,8},{24,0},{1,25},{9,17},{17,9},{25,1},{2,26},{10... | collective-permute-start | bytes 319496 | tf_op jit(solution)/shard_map/ppermute | solution.py:365
  16.4 0.5 %collective-permute-start.9 = (bf16[2,208,128]{2,1,0:T(8,128)(2,1)S(1)}, bf16[2,208,128]{2,1,0:T(8,128)(2,1)S(1)}, u32[]{:S(2)}, u32[]{:S(2)}) collective-permute-start(bf16[2,208,128]{2,1,0:T(8,128)(2,1)S(1)} %collective-permute-done.1.refs_1_), channel_id=1, source_target_pairs={{0,2},{2,0},{1,3},{3,1},{4,6},{6,4},{5,7},{7,5},{8,10},{10,8},{9,1... | collective-permute-start | bytes 319496 | tf_op jit(solution)/shard_map/ppermute | solution.py:365
  17.0 1.7 %collective-permute-done.6.refs_5_ = bf16[2,208,128]{2,1,0:T(8,128)(2,1)S(1)} collective-permute-done((bf16[2,208,128]{2,1,0:T(8,128)(2,1)S(1)}, bf16[2,208,128]{2,1,0:T(8,128)(2,1)S(1)}, u32[]{:S(2)}, u32[]{:S(2)}) %collective-permute-start.6) | collective-permute-done | bytes 106528 | tf_op jit(solution)/shard_map/ppermute | solution.py:365
  18.7 0.7 %collective-permute-done.3.refs_2_ = bf16[2,208,128]{2,1,0:T(8,128)(2,1)S(1)} collective-permute-done((bf16[2,208,128]{2,1,0:T(8,128)(2,1)S(1)}, bf16[2,208,128]{2,1,0:T(8,128)(2,1)S(1)}, u32[]{:S(2)}, u32[]{:S(2)}) %collective-permute-start.3) | collective-permute-done | bytes 106528 | tf_op jit(solution)/shard_map/ppermute | solution.py:365
  19.4 2.8 %collective-permute-done.4.refs_3_ = bf16[2,208,128]{2,1,0:T(8,128)(2,1)S(1)} collective-permute-done((bf16[2,208,128]{2,1,0:T(8,128)(2,1)S(1)}, bf16[2,208,128]{2,1,0:T(8,128)(2,1)S(1)}, u32[]{:S(2)}, u32[]{:S(2)}) %collective-permute-start.4) | collective-permute-done | bytes 106528 | tf_op jit(solution)/shard_map/ppermute | solution.py:365
  22.2 0.6 %collective-permute-start.12 = (bf16[2,208,128]{2,1,0:T(8,128)(2,1)S(1)}, bf16[2,208,128]{2,1,0:T(8,128)(2,1)S(1)}, u32[]{:S(2)}, u32[]{:S(2)}) collective-permute-start(bf16[2,208,128]{2,1,0:T(8,128)(2,1)S(1)} %collective-permute-done.3.refs_2_), channel_id=1, source_target_pairs={{0,2},{2,0},{1,3},{3,1},{4,6},{6,4},{5,7},{7,5},{8,10},{10,8},{9,1... | collective-permute-start | bytes 319496 | tf_op jit(solution)/shard_map/ppermute | solution.py:365
  22.7 1.5 %collective-permute-start.15 = (bf16[2,208,128]{2,1,0:T(8,128)(2,1)S(1)}, bf16[2,208,128]{2,1,0:T(8,128)(2,1)S(1)}, u32[]{:S(2)}, u32[]{:S(2)}) collective-permute-start(bf16[2,208,128]{2,1,0:T(8,128)(2,1)S(1)} %collective-permute-done.4.refs_3_), channel_id=1, source_target_pairs={{0,2},{2,0},{1,3},{3,1},{4,6},{6,4},{5,7},{7,5},{8,10},{10,8},{9,1... | collective-permute-start | bytes 319496 | tf_op jit(solution)/shard_map/ppermute | solution.py:365
  24.2 0.5 %collective-permute-start.11 = (bf16[2,208,128]{2,1,0:T(8,128)(2,1)S(1)}, bf16[2,208,128]{2,1,0:T(8,128)(2,1)S(1)}, u32[]{:S(2)}, u32[]{:S(2)}) collective-permute-start(bf16[2,208,128]{2,1,0:T(8,128)(2,1)S(1)} %collective-permute-done.3.refs_2_), channel_id=1, source_target_pairs={{0,4},{4,0},{1,5},{5,1},{2,6},{6,2},{3,7},{7,3},{8,12},{12,8},{9,1... | collective-permute-start | bytes 319496 | tf_op jit(solution)/shard_map/ppermute | solution.py:365
  24.8 3.1 %collective-permute-done.12.refs_5_ = bf16[2,208,128]{2,1,0:T(8,128)(2,1)S(1)} collective-permute-done((bf16[2,208,128]{2,1,0:T(8,128)(2,1)S(1)}, bf16[2,208,128]{2,1,0:T(8,128)(2,1)S(1)}, u32[]{:S(2)}, u32[]{:S(2)}) %collective-permute-start.12) | collective-permute-done | bytes 106528 | tf_op jit(solution)/shard_map/ppermute | solution.py:365
  27.9 1.1 %collective-permute-done.15.refs_8_ = bf16[2,208,128]{2,1,0:T(8,128)(2,1)S(1)} collective-permute-done((bf16[2,208,128]{2,1,0:T(8,128)(2,1)S(1)}, bf16[2,208,128]{2,1,0:T(8,128)(2,1)S(1)}, u32[]{:S(2)}, u32[]{:S(2)}) %collective-permute-start.15) | collective-permute-done | bytes 106528 | tf_op jit(solution)/shard_map/ppermute | solution.py:365
  29.0 0.6 %match_first.1 = (bf16[272,768]{1,0:T(8,128)(2,1)S(1)}, f32[272,128]{1,0:T(8,128)S(1)}, f32[272,128]{1,0:T(8,128)S(1)}, f32[272,128]{1,0:T(8,128)S(1)}) custom-call(bf16[2,208,128]{2,1,0:T(8,128)(2,1)S(1)} %pad_maximum_fusion.refs_0_, bf16[2,208,128]{2,1,0:T(8,128)(2,1)S(1)} %collective-permute-done.1.refs_1_, ...), custom_call_target="tpu_custom_call" | custom-call | flops 106954752 | bytes 425984 | tf_op jit(solution)/shard_map/match_first/pallas_call | solution.py:306
  29.6 0.6 %match_next.2.refs_3_ = f32[272,128]{1,0:T(8,128)S(1)} custom-call(bf16[272,768]{1,0:T(8,128)(2,1)S(1)} %get-tuple-element.23.refs_0_, f32[272,128]{1,0:T(8,128)S(1)} %get-tuple-element.24.refs_1_, f32[272,128]{1,0:T(8,128)S(1)} %get-tuple-element.25.refs_2_, f32[272,128]{1,0:T(8,128)S(1)} %get-tuple-element.26.refs_3_, ...), custom_call_target="tpu_custom_call" | custom-call | flops 160432128 | bytes 638976 | tf_op jit(solution)/shard_map/match_next/pallas_call | solution.py:324
  30.3 0.7 %match_next.3 = f32[8,1,128]{2,1,0:T(1,128)S(1)} custom-call(bf16[272,768]{1,0:T(8,128)(2,1)S(1)} %get-tuple-element.23.refs_0_, f32[272,128]{1,0:T(8,128)S(1)} %get-tuple-element.24.refs_1_, f32[272,128]{1,0:T(8,128)S(1)} %get-tuple-element.25.refs_2_, f32[272,128]{1,0:T(8,128)S(1)} %match_next.2.refs_3_, ...), custom_call_target="tpu_custom_call" | custom-call | flops 160432128 | bytes 638976 | tf_op jit(solution)/shard_map/match_next/pallas_call | solution.py:324
  31.0 11.9 %all_to_all.5.best_ref = f32[8,1,128]{2,1,0:T(1,128)} all-to-all(f32[8,1,128]{2,1,0:T(1,128)S(1)} %match_next.3), channel_id=1, replica_groups=mesh['z'=4,'core'=2,'y'=2,'x'=2] {'z','x'}, dimensions={0} | all-to-all | bytes 8192 | tf_op jit(solution)/shard_map/all_to_all | solution.py:399
  42.9 1.4 %collect.1 = f32[2,128]{1,0:T(2,128)} custom-call(s32[2,256]{1,0:T(2,128)} %copy-done.1, f32[8,1,128]{2,1,0:T(1,128)} %all_to_all.5.best_ref), custom_call_target="tpu_custom_call" | custom-call | tf_op jit(solution)/shard_map/collect/pallas_call | solution.py:355
  (30 shorter events, 0.3 us)
Async XLA Ops:
  0.0 0.7 %copy-start.3 = (s32[256]{0:T(256)S(1)}, s32[256]{0:T(256)}, u32[]{:S(2)}) copy-start(s32[256]{0:T(256)} %param.5) | copy-start | bytes 3076
  0.0 0.7 %copy-start.2 = (s32[256]{0:T(256)S(1)}, s32[256]{0:T(256)}, u32[]{:S(2)}) copy-start(s32[256]{0:T(256)} %param.4) | copy-start | bytes 3076
  0.7 1.0 %copy-start = (bf16[256,768]{1,0:T(8,128)(2,1)S(1)}, bf16[256,768]{1,0:T(8,128)(2,1)}, u32[]{:S(2)}) copy-start(bf16[256,768]{1,0:T(8,128)(2,1)} %embed_ref.1) | copy-start | bytes 1179652
  2.2 6.8 %copy-start.1 = (s32[2,256]{1,0:T(2,128)}, s32[2,256]{1,0:T(2,128)S(1)}, u32[]{:S(2)}) copy-start(s32[2,256]{1,0:T(2,128)S(1)} %get-tuple-element.16.info_ref) | copy-start | bytes 6148
  2.2 6.8 %collective-permute-start = (bf16[2,208,128]{2,1,0:T(8,128)(2,1)S(1)}, bf16[2,208,128]{2,1,0:T(8,128)(2,1)S(1)}, u32[]{:S(2)}, u32[]{:S(2)}) collective-permute-start(bf16[2,208,128]{2,1,0:T(8,128)(2,1)S(1)} %get-tuple-element.18), channel_id=1, source_target_pairs={{0,1},{1,0},{2,3},{3,2},{4,5},{5,4},{6,7},{7,6},{8,9},{9,8},{10,11... | collective-permute-start | bytes 319496 | tf_op jit(solution)/shard_map/ppermute | solution.py:365
  5.2 6.0 %collective-permute-start.2 = (bf16[2,208,128]{2,1,0:T(8,128)(2,1)S(1)}, bf16[2,208,128]{2,1,0:T(8,128)(2,1)S(1)}, u32[]{:S(2)}, u32[]{:S(2)}) collective-permute-start(bf16[2,208,128]{2,1,0:T(8,128)(2,1)S(1)} %get-tuple-element.21), channel_id=1, source_target_pairs={{0,1},{1,0},{2,3},{3,2},{4,5},{5,4},{6,7},{7,6},{8,9},{9,8},{10,11... | collective-permute-start | bytes 319496 | tf_op jit(solution)/shard_map/ppermute | solution.py:365
  9.1 7.4 %collective-permute-start.1 = (bf16[2,208,128]{2,1,0:T(8,128)(2,1)S(1)}, bf16[2,208,128]{2,1,0:T(8,128)(2,1)S(1)}, u32[]{:S(2)}, u32[]{:S(2)}) collective-permute-start(bf16[2,208,128]{2,1,0:T(8,128)(2,1)S(1)} %pad_maximum_fusion.1), channel_id=1, source_target_pairs={{0,8},{8,0},{16,24},{24,16},{1,9},{9,1},{17,25},{25,17},{2,10},{10... | collective-permute-start | bytes 319496 | tf_op jit(solution)/shard_map/ppermute | solution.py:365
  11.2 8.1 %collective-permute-start.3 = (bf16[2,208,128]{2,1,0:T(8,128)(2,1)S(1)}, bf16[2,208,128]{2,1,0:T(8,128)(2,1)S(1)}, u32[]{:S(2)}, u32[]{:S(2)}) collective-permute-start(bf16[2,208,128]{2,1,0:T(8,128)(2,1)S(1)} %pad_maximum_fusion.2), channel_id=1, source_target_pairs={{0,16},{8,24},{16,0},{24,8},{1,17},{9,25},{17,1},{25,9},{2,18},{10... | collective-permute-start | bytes 319496 | tf_op jit(solution)/shard_map/ppermute | solution.py:365
  13.9 4.8 %collective-permute-start.6 = (bf16[2,208,128]{2,1,0:T(8,128)(2,1)S(1)}, bf16[2,208,128]{2,1,0:T(8,128)(2,1)S(1)}, u32[]{:S(2)}, u32[]{:S(2)}) collective-permute-start(bf16[2,208,128]{2,1,0:T(8,128)(2,1)S(1)} %pad_maximum_fusion.refs_0_), channel_id=1, source_target_pairs={{0,2},{2,0},{1,3},{3,1},{4,6},{6,4},{5,7},{7,5},{8,10},{10,8},{9,1... | collective-permute-start | bytes 319496 | tf_op jit(solution)/shard_map/ppermute | solution.py:365
  15.5 6.7 %collective-permute-start.4 = (bf16[2,208,128]{2,1,0:T(8,128)(2,1)S(1)}, bf16[2,208,128]{2,1,0:T(8,128)(2,1)S(1)}, u32[]{:S(2)}, u32[]{:S(2)}) collective-permute-start(bf16[2,208,128]{2,1,0:T(8,128)(2,1)S(1)} %pad_maximum_fusion.3), channel_id=1, source_target_pairs={{0,24},{8,16},{16,8},{24,0},{1,25},{9,17},{17,9},{25,1},{2,26},{10... | collective-permute-start | bytes 319496 | tf_op jit(solution)/shard_map/ppermute | solution.py:365
  16.4 6.3 %collective-permute-start.5 = (bf16[2,208,128]{2,1,0:T(8,128)(2,1)S(1)}, bf16[2,208,128]{2,1,0:T(8,128)(2,1)S(1)}, u32[]{:S(2)}, u32[]{:S(2)}) collective-permute-start(bf16[2,208,128]{2,1,0:T(8,128)(2,1)S(1)} %pad_maximum_fusion.refs_0_), channel_id=1, source_target_pairs={{0,4},{4,0},{1,5},{5,1},{2,6},{6,2},{3,7},{7,3},{8,12},{12,8},{9,1... | collective-permute-start | bytes 319496 | tf_op jit(solution)/shard_map/ppermute | solution.py:365
  16.4 7.8 %collective-permute-start.9 = (bf16[2,208,128]{2,1,0:T(8,128)(2,1)S(1)}, bf16[2,208,128]{2,1,0:T(8,128)(2,1)S(1)}, u32[]{:S(2)}, u32[]{:S(2)}) collective-permute-start(bf16[2,208,128]{2,1,0:T(8,128)(2,1)S(1)} %collective-permute-done.1.refs_1_), channel_id=1, source_target_pairs={{0,2},{2,0},{1,3},{3,1},{4,6},{6,4},{5,7},{7,5},{8,10},{10,8},{9,1... | collective-permute-start | bytes 319496 | tf_op jit(solution)/shard_map/ppermute | solution.py:365
  18.7 5.5 %collective-permute-start.7 = (bf16[2,208,128]{2,1,0:T(8,128)(2,1)S(1)}, bf16[2,208,128]{2,1,0:T(8,128)(2,1)S(1)}, u32[]{:S(2)}, u32[]{:S(2)}) collective-permute-start(bf16[2,208,128]{2,1,0:T(8,128)(2,1)S(1)} %collective-permute-done.6.refs_5_), channel_id=1, source_target_pairs={{0,4},{4,0},{1,5},{5,1},{2,6},{6,2},{3,7},{7,3},{8,12},{12,8},{9,1... | collective-permute-start | bytes 319496 | tf_op jit(solution)/shard_map/ppermute | solution.py:365
  19.4 5.4 %collective-permute-start.8 = (bf16[2,208,128]{2,1,0:T(8,128)(2,1)S(1)}, bf16[2,208,128]{2,1,0:T(8,128)(2,1)S(1)}, u32[]{:S(2)}, u32[]{:S(2)}) collective-permute-start(bf16[2,208,128]{2,1,0:T(8,128)(2,1)S(1)} %collective-permute-done.1.refs_1_), channel_id=1, source_target_pairs={{0,4},{4,0},{1,5},{5,1},{2,6},{6,2},{3,7},{7,3},{8,12},{12,8},{9,1... | collective-permute-start | bytes 319496 | tf_op jit(solution)/shard_map/ppermute | solution.py:365
  22.2 5.7 %collective-permute-start.12 = (bf16[2,208,128]{2,1,0:T(8,128)(2,1)S(1)}, bf16[2,208,128]{2,1,0:T(8,128)(2,1)S(1)}, u32[]{:S(2)}, u32[]{:S(2)}) collective-permute-start(bf16[2,208,128]{2,1,0:T(8,128)(2,1)S(1)} %collective-permute-done.3.refs_2_), channel_id=1, source_target_pairs={{0,2},{2,0},{1,3},{3,1},{4,6},{6,4},{5,7},{7,5},{8,10},{10,8},{9,1... | collective-permute-start | bytes 319496 | tf_op jit(solution)/shard_map/ppermute | solution.py:365
  22.7 6.2 %collective-permute-start.15 = (bf16[2,208,128]{2,1,0:T(8,128)(2,1)S(1)}, bf16[2,208,128]{2,1,0:T(8,128)(2,1)S(1)}, u32[]{:S(2)}, u32[]{:S(2)}) collective-permute-start(bf16[2,208,128]{2,1,0:T(8,128)(2,1)S(1)} %collective-permute-done.4.refs_3_), channel_id=1, source_target_pairs={{0,2},{2,0},{1,3},{3,1},{4,6},{6,4},{5,7},{7,5},{8,10},{10,8},{9,1... | collective-permute-start | bytes 319496 | tf_op jit(solution)/shard_map/ppermute | solution.py:365
  24.2 5.4 %collective-permute-start.10 = (bf16[2,208,128]{2,1,0:T(8,128)(2,1)S(1)}, bf16[2,208,128]{2,1,0:T(8,128)(2,1)S(1)}, u32[]{:S(2)}, u32[]{:S(2)}) collective-permute-start(bf16[2,208,128]{2,1,0:T(8,128)(2,1)S(1)} %collective-permute-done.9.refs_8_), channel_id=1, source_target_pairs={{0,4},{4,0},{1,5},{5,1},{2,6},{6,2},{3,7},{7,3},{8,12},{12,8},{9,1... | collective-permute-start | bytes 319496 | tf_op jit(solution)/shard_map/ppermute | solution.py:365
  24.2 6.0 %collective-permute-start.11 = (bf16[2,208,128]{2,1,0:T(8,128)(2,1)S(1)}, bf16[2,208,128]{2,1,0:T(8,128)(2,1)S(1)}, u32[]{:S(2)}, u32[]{:S(2)}) collective-permute-start(bf16[2,208,128]{2,1,0:T(8,128)(2,1)S(1)} %collective-permute-done.3.refs_2_), channel_id=1, source_target_pairs={{0,4},{4,0},{1,5},{5,1},{2,6},{6,2},{3,7},{7,3},{8,12},{12,8},{9,1... | collective-permute-start | bytes 319496 | tf_op jit(solution)/shard_map/ppermute | solution.py:365
  24.7 5.5 %collective-permute-start.14 = (bf16[2,208,128]{2,1,0:T(8,128)(2,1)S(1)}, bf16[2,208,128]{2,1,0:T(8,128)(2,1)S(1)}, u32[]{:S(2)}, u32[]{:S(2)}) collective-permute-start(bf16[2,208,128]{2,1,0:T(8,128)(2,1)S(1)} %collective-permute-done.4.refs_3_), channel_id=1, source_target_pairs={{0,4},{4,0},{1,5},{5,1},{2,6},{6,2},{3,7},{7,3},{8,12},{12,8},{9,1... | collective-permute-start | bytes 319496 | tf_op jit(solution)/shard_map/ppermute | solution.py:365
  27.8 2.4 %collective-permute-start.13 = (bf16[2,208,128]{2,1,0:T(8,128)(2,1)S(1)}, bf16[2,208,128]{2,1,0:T(8,128)(2,1)S(1)}, u32[]{:S(2)}, u32[]{:S(2)}) collective-permute-start(bf16[2,208,128]{2,1,0:T(8,128)(2,1)S(1)} %collective-permute-done.12.refs_5_), channel_id=1, source_target_pairs={{0,4},{4,0},{1,5},{5,1},{2,6},{6,2},{3,7},{7,3},{8,12},{12,8},{9,1... | collective-permute-start | bytes 319496 | tf_op jit(solution)/shard_map/ppermute | solution.py:365
  29.0 1.3 %collective-permute-start.16 = (bf16[2,208,128]{2,1,0:T(8,128)(2,1)S(1)}, bf16[2,208,128]{2,1,0:T(8,128)(2,1)S(1)}, u32[]{:S(2)}, u32[]{:S(2)}) collective-permute-start(bf16[2,208,128]{2,1,0:T(8,128)(2,1)S(1)} %collective-permute-done.15.refs_8_), channel_id=1, source_target_pairs={{0,4},{4,0},{1,5},{5,1},{2,6},{6,2},{3,7},{7,3},{8,12},{12,8},{9,1... | collective-permute-start | bytes 319496 | tf_op jit(solution)/shard_map/ppermute | solution.py:365

commit v2 on v1

--- a/solution.py
+++ b/solution.py
@@ -79,7 +79,14 @@
     return lax.dot_general(left, right, (contract, ((), ())), preferred_element_type=jnp.float32)
 
 
-def place_kernel(s, layout, embed_ref, cluster_ref, rank_ref, info_ref, *out_refs):
+def place_kernel(s, layout, embed_hbm, cluster_hbm, rank_hbm, info_ref, *refs):
+    out_refs, (embed_ref, cluster_ref, rank_ref, arrival) = refs[: len(layout)], refs[len(layout) :]
+    pairs = ((embed_hbm, embed_ref), (cluster_hbm, cluster_ref), (rank_hbm, rank_ref))
+    copies = [pltpu.make_async_copy(src, dst, arrival.at[i]) for i, (src, dst) in enumerate(pairs)]
+    for copy in copies:
+        copy.start()
+    for copy in copies:
+        copy.wait()
     widened = embed_ref[...].astype(jnp.float32)
     total = jnp.sum(widened * widened, axis=1, keepdims=True)
     unit = (widened * lax.rsqrt(total + 1e-06)).astype(jnp.bfloat16)
@@ -124,14 +131,22 @@
 
 
 def place(s, layout, embed, cluster, rank):
+    inputs = (embed, cluster.reshape(-1, LANES), rank.reshape(-1, LANES))
     outs = [jax.ShapeDtypeStruct((2, s.rows), jnp.int32)]
     outs += [jax.ShapeDtypeStruct((len(m), s.block_rows, LANES), jnp.bfloat16) for m in layout]
     return pl.pallas_call(
         functools.partial(place_kernel, s, layout),
         out_shape=outs,
+        in_specs=[pl.BlockSpec(memory_space=pltpu.HBM)] * 3,
+        scratch_shapes=[
+            pltpu.VMEM(embed.shape, embed.dtype),
+            pltpu.VMEM((s.rows // LANES, LANES), jnp.int32),
+            pltpu.VMEM((s.rows // LANES, LANES), jnp.int32),
+            pltpu.SemaphoreType.DMA((3,)),
+        ],
         compiler_params=pltpu.CompilerParams(vmem_limit_bytes=VMEM_LIMIT),
         name="place",
-    )(embed, cluster.reshape(-1, LANES), rank.reshape(-1, LANES))
+    )(*(pltpu.with_memory_space_constraint(a, pltpu.HBM) for a in inputs))
 
 
 def blocks_of(refs):
@@ -355,6 +370,7 @@
     out = pl.pallas_call(
         functools.partial(collect_kernel, s),
         out_shape=jax.ShapeDtypeStruct((s.rows // LANES, LANES), jnp.float32),
+        compiler_params=pltpu.CompilerParams(vmem_limit_bytes=8 * 1024 * 1024),
         name="collect",
     )(info, best)
     return out.reshape(s.rows)
@@ -367,30 +383,22 @@
 
 def local(embed, cluster, rank):
     s = Shape(embed.shape[0], embed.shape[1], lax.axis_size("z"), lax.axis_size("x"), lax.axis_size("y"))
-    own = [[s.x * k] for k in range(s.z)]
-    far = [s.x * k + 1 for k in range(s.z // 2, s.z)]
-    near = [s.x * k + 1 for k in range(s.z // 2)]
-    info, *arrays = place(s, own + [far, near], embed, cluster, rank)
-    owned, (far_rows, near_rows) = arrays[: s.z], arrays[s.z :]
-    crossed = jnp.concatenate([swap(near_rows, "x", 1), swap(far_rows, "x", 1)])
-    arrived = [
-        jnp.concatenate([owned[k], crossed[k : k + 1]]) for k in range(s.z)
-    ]
-    arrived = [swap(a, "z", k) if k else a for k, a in enumerate(arrived)]
     order = [s.x * k + j for k in range(s.z) for j in range(s.x)]
+    info, *blocks = place(s, [[s.x * k + j for j in range(s.x)] for k in range(s.z)], embed, cluster, rank)
+    arrived = {k: swap(blocks[k], "z", k) if k else blocks[k] for k in reversed(range(s.z))}
+    near = swap(jnp.concatenate([arrived[0][1:], arrived[1][1:]]), "x", 1)
+    queries = [jnp.concatenate([arrived[0][:1], near[:1], arrived[1][:1], near[1:]])]
+    queries += [jnp.concatenate([arrived[k][:1], swap(arrived[k][1:], "x", 1)]) for k in range(2, s.z)]
+    state = match_first(s, order, queries, [], False)
     if s.y == 2:
         waves = []
-        for a in arrived:
+        for a in queries:
             over = swap(a, "y", 1)
-            waves.append([swap(a, "core", 1), over, swap(over, "core", 1)])
-        state = match_first(s, order, arrived, [], False)
-        for i, keys in enumerate(waves):
-            if i % 2 == 1:
-                state = match_next(s, order, state, waves[i - 1] + keys, i == len(waves) - 1)
+            waves.append([over, swap(jnp.concatenate([a, over]), "core", 1)])
+        state = match_next(s, order, state, waves[0], False)
+        state = match_next(s, order, state, [a for wave in waves[1:] for a in wave], True)
     else:
-        both = jnp.concatenate(arrived)
-        everyone = lax.all_gather(both, ("core", "y"), axis=0)
-        state = match_first(s, order, [both], [], False)
+        everyone = lax.all_gather(jnp.concatenate(queries), ("core", "y"), axis=0)
         me = lax.axis_index(("core", "y"))
         size = everyone.shape[0]
         for i in range(1, size):

time: 44.5 us -> 41.2 us (0.926)
  blocking collectives: 11.9 us -> 10.2 us
  local copies, waits for them, and re-layouts: 1.71 us -> 0.12 us
    all_to_all x1, blocking collectives: 11.9 us -> 10.2 us  [local(): lax.all_to_all(state[3], ('z', 'x'), split_axis=0, concat_axis=0, tiled=T...]
    unnamed x8 -> x4, local copies, waits for them, and re-layouts: 1.69 us -> 0.07 us
    pallas_call x1, Pallas kernels: 0.51 us -> 1.53 us  [place(): pl.pallas_call(functools.partial(place_kernel, s, layout), out_shape=outs...]
    pallas_call x1, Pallas kernels: 1.4 us -> 0.71 us  [collect(): pl.pallas_call(functools.partial(collect_kernel, s), out_shape=jax.ShapeD...]
    ppermute x17 -> x12, waiting for transfers between devices: 13.2 us -> 12.8 us  [swap(): return lax.ppermute(array, axis, [(i, i ^ flip) for i in range(size)])]
    ppermute x17 -> x12, starting transfers between devices: 13.5 us -> 13.5 us  [swap(): return lax.ppermute(array, axis, [(i, i ^ flip) for i in range(size)])]
  transfers between devices with their start and end apart: 17 -> 12, of which waited for: 7 -> 7; matrix products, arithmetic and copies ran while one was open for 0% -> 1% of each run, Pallas kernels for 3% -> 3%
where the time goes in v2:
time: 41.2 us; the launch traced here: 41.1 us
  starting transfers between devices  13.5 us (33%)
  waiting for transfers between devices  12.8 us (31%)
  blocking collectives  10.2 us (25%)
  Pallas kernels  4.17 us (10%)
    ppermute x12, starting transfers between devices, swap(): return lax.ppermute(array, axis, [(i, i ^ flip) for i in range(size)])  13.5 us
    ppermute x12, waiting for transfers between devices, swap(): return lax.ppermute(array, axis, [(i, i ^ flip) for i in range(size)])  12.8 us
    all_to_all x1, blocking collectives, local(): lax.all_to_all(state[3], ('z', 'x'), split_axis=0, concat_axis=0, tiled=T...  10.2 us
    pallas_call x1, Pallas kernels, place(): pl.pallas_call(functools.partial(place_kernel, s, layout), out_shape=outs...  1.53 us
    pallas_call x2, Pallas kernels, match_next(): pl.pallas_call(functools.partial(next_kernel, s, order, len(keys), last),...  1.33 us
  transfers between devices with their start and end apart: 12, of which 7 were waited for; matrix products, arithmetic and copies ran while one was open for 1% of the time, Pallas kernels for 3%

profile of v2, /device:TPU:0, one launch (start us, length us, event | category | flops | bytes accessed | tf_op | source)
XLA Modules:
  0.0 41.1 jit_solution(9781889802028503820)
XLA Ops:
  0.0 1.5 %place.1 = (s32[2,256]{1,0:T(2,128)S(1)}, bf16[2,208,128]{2,1,0:T(8,128)(2,1)S(1)}, bf16[2,208,128]{2,1,0:T(8,128)(2,1)S(1)}, bf16[2,208,128]{2,1,0:T(8,128)(2,1)S(1)}, bf16[2,208,128]{2,1,0:T(8,128)(2,1)S(1)}) custom-call(bf16[256,768]{1,0:T(8,128)(2,1)} %embed_hbm.1, s32[2,128]{1,0:T(2,128)} %bitcast.3, s32[2,128]{1,0:T(2,128)} %bitcast.4), custom_call_target="tpu_custom_call" | custom-call | tf_op jit(solution)/shard_map/place/pallas_call | solution.py:137
  1.5 3.1 %collective-permute-start = (bf16[2,208,128]{2,1,0:T(8,128)(2,1)S(1)}, bf16[2,208,128]{2,1,0:T(8,128)(2,1)S(1)}, u32[]{:S(2)}, u32[]{:S(2)}) collective-permute-start(bf16[2,208,128]{2,1,0:T(8,128)(2,1)S(1)} %get-tuple-element.16), channel_id=1, source_target_pairs={{0,8},{8,0},{16,24},{24,16},{1,9},{9,1},{17,25},{25,17},{2,10},{10... | collective-permute-start | bytes 319496 | tf_op jit(solution)/shard_map/ppermute | solution.py:381
  4.6 2.6 %collective-permute-start.2 = (bf16[2,208,128]{2,1,0:T(8,128)(2,1)S(1)}, bf16[2,208,128]{2,1,0:T(8,128)(2,1)S(1)}, u32[]{:S(2)}, u32[]{:S(2)}) collective-permute-start(bf16[2,208,128]{2,1,0:T(8,128)(2,1)S(1)} %get-tuple-element.17), channel_id=1, source_target_pairs={{0,16},{8,24},{16,0},{24,8},{1,17},{9,25},{17,1},{25,9},{2,18},{10... | collective-permute-start | bytes 319496 | tf_op jit(solution)/shard_map/ppermute | solution.py:381
  7.2 0.4 collective-permute-done
  7.6 1.7 %collective-permute-start.1 = (bf16[2,208,128]{2,1,0:T(8,128)(2,1)S(1)}, bf16[2,208,128]{2,1,0:T(8,128)(2,1)S(1)}, u32[]{:S(2)}, u32[]{:S(2)}) collective-permute-start(bf16[2,208,128]{2,1,0:T(8,128)(2,1)S(1)} %pad_maximum_fusion.3), channel_id=1, source_target_pairs={{0,1},{1,0},{2,3},{3,2},{4,5},{5,4},{6,7},{7,6},{8,9},{9,8},{10,11... | collective-permute-start | bytes 319496 | tf_op jit(solution)/shard_map/ppermute | solution.py:381
  9.4 6.3 %collective-permute-done.2 = bf16[2,208,128]{2,1,0:T(8,128)(2,1)S(1)} collective-permute-done((bf16[2,208,128]{2,1,0:T(8,128)(2,1)S(1)}, bf16[2,208,128]{2,1,0:T(8,128)(2,1)S(1)}, u32[]{:S(2)}, u32[]{:S(2)}) %collective-permute-start.2) | collective-permute-done | bytes 106528 | tf_op jit(solution)/shard_map/ppermute | solution.py:381
  15.7 1.6 %collective-permute-start.3 = (bf16[1,208,128]{2,1,0:T(8,128)(2,1)S(1)}, bf16[1,208,128]{2,1,0:T(8,128)(2,1)S(1)}, u32[]{:S(2)}, u32[]{:S(2)}) collective-permute-start(bf16[1,208,128]{2,1,0:T(8,128)(2,1)S(1)} %get-tuple-element.34), channel_id=1, source_target_pairs={{0,1},{1,0},{2,3},{3,2},{4,5},{5,4},{6,7},{7,6},{8,9},{9,8},{10,11... | collective-permute-start | bytes 159752 | tf_op jit(solution)/shard_map/ppermute | solution.py:381
  17.3 0.6 %collective-permute-start.5 = (bf16[1,208,128]{2,1,0:T(8,128)(2,1)S(1)}, bf16[1,208,128]{2,1,0:T(8,128)(2,1)S(1)}, u32[]{:S(2)}, u32[]{:S(2)}) collective-permute-start(bf16[1,208,128]{2,1,0:T(8,128)(2,1)S(1)} %get-tuple-element.32), channel_id=1, source_target_pairs={{0,1},{1,0},{2,3},{3,2},{4,5},{5,4},{6,7},{7,6},{8,9},{9,8},{10,11... | collective-permute-start | bytes 159752 | tf_op jit(solution)/shard_map/ppermute | solution.py:381
  18.0 1.6 %collective-permute-start.6 = (bf16[4,208,128]{2,1,0:T(8,128)(2,1)S(1)}, bf16[4,208,128]{2,1,0:T(8,128)(2,1)S(1)}, u32[]{:S(2)}, u32[]{:S(2)}) collective-permute-start(bf16[4,208,128]{2,1,0:T(8,128)(2,1)S(1)} %pad_maximum_fusion.refs_0_), channel_id=1, source_target_pairs={{0,2},{2,0},{1,3},{3,1},{4,6},{6,4},{5,7},{7,5},{8,10},{10,8},{9,1... | collective-permute-start | bytes 638984 | tf_op jit(solution)/shard_map/ppermute | solution.py:381
  19.6 1.9 %collective-permute-done.5 = bf16[1,208,128]{2,1,0:T(8,128)(2,1)S(1)} collective-permute-done((bf16[1,208,128]{2,1,0:T(8,128)(2,1)S(1)}, bf16[1,208,128]{2,1,0:T(8,128)(2,1)S(1)}, u32[]{:S(2)}, u32[]{:S(2)}) %collective-permute-start.5) | collective-permute-done | bytes 53280 | tf_op jit(solution)/shard_map/ppermute | solution.py:381
  21.5 1.6 %collective-permute-start.10 = (bf16[2,208,128]{2,1,0:T(8,128)(2,1)S(1)}, bf16[2,208,128]{2,1,0:T(8,128)(2,1)S(1)}, u32[]{:S(2)}, u32[]{:S(2)}) collective-permute-start(bf16[2,208,128]{2,1,0:T(8,128)(2,1)S(1)} %pad_maximum_fusion.5.refs_2_), channel_id=1, source_target_pairs={{0,2},{2,0},{1,3},{3,1},{4,6},{6,4},{5,7},{7,5},{8,10},{10,8},{9,1... | collective-permute-start | bytes 319496 | tf_op jit(solution)/shard_map/ppermute | solution.py:381
  23.1 0.6 %collective-permute-start.8 = (bf16[2,208,128]{2,1,0:T(8,128)(2,1)S(1)}, bf16[2,208,128]{2,1,0:T(8,128)(2,1)S(1)}, u32[]{:S(2)}, u32[]{:S(2)}) collective-permute-start(bf16[2,208,128]{2,1,0:T(8,128)(2,1)S(1)} %pad_maximum_fusion.4.refs_1_), channel_id=1, source_target_pairs={{0,2},{2,0},{1,3},{3,1},{4,6},{6,4},{5,7},{7,5},{8,10},{10,8},{9,1... | collective-permute-start | bytes 319496 | tf_op jit(solution)/shard_map/ppermute | solution.py:381
  23.7 0.3 collective-permute-done.6.refs_4_
  24.0 0.1 collective-permute-start.7
  24.0 2.2 %collective-permute-done.10.refs_6_ = bf16[2,208,128]{2,1,0:T(8,128)(2,1)S(1)} collective-permute-done((bf16[2,208,128]{2,1,0:T(8,128)(2,1)S(1)}, bf16[2,208,128]{2,1,0:T(8,128)(2,1)S(1)}, u32[]{:S(2)}, u32[]{:S(2)}) %collective-permute-start.10) | collective-permute-done | bytes 106528 | tf_op jit(solution)/shard_map/ppermute | solution.py:381
  26.3 0.1 collective-permute-start.11
  26.4 1.5 %collective-permute-done.8.refs_4_ = bf16[2,208,128]{2,1,0:T(8,128)(2,1)S(1)} collective-permute-done((bf16[2,208,128]{2,1,0:T(8,128)(2,1)S(1)}, bf16[2,208,128]{2,1,0:T(8,128)(2,1)S(1)}, u32[]{:S(2)}, u32[]{:S(2)}) %collective-permute-start.8) | collective-permute-done | bytes 106528 | tf_op jit(solution)/shard_map/ppermute | solution.py:381
  27.9 0.1 collective-permute-start.9
  28.0 0.6 %match_first.1 = (bf16[272,768]{1,0:T(8,128)(2,1)S(1)}, f32[272,128]{1,0:T(8,128)S(1)}, f32[272,128]{1,0:T(8,128)S(1)}, f32[272,128]{1,0:T(8,128)S(1)}) custom-call(bf16[4,208,128]{2,1,0:T(8,128)(2,1)S(1)} %pad_maximum_fusion.refs_0_, bf16[2,208,128]{2,1,0:T(8,128)(2,1)S(1)} %pad_maximum_fusion.4.refs_1_, bf16[2,208,128]{2,1,0:T(8,128)(2,1)S(1)} %pad_maximum_fusion.5.refs_2_), custom_call_target="tpu_custom_call" | custom-call | flops 106954752 | bytes 425984 | tf_op jit(solution)/shard_map/match_first/pallas_call | solution.py:321
  28.6 0.6 %match_next.2.refs_3_ = f32[272,128]{1,0:T(8,128)S(1)} custom-call(bf16[272,768]{1,0:T(8,128)(2,1)S(1)} %get-tuple-element.19.refs_0_, f32[272,128]{1,0:T(8,128)S(1)} %get-tuple-element.20.refs_1_, f32[272,128]{1,0:T(8,128)S(1)} %get-tuple-element.21.refs_2_, f32[272,128]{1,0:T(8,128)S(1)} %get-tuple-element.22.refs_3_, ...), custom_call_target="tpu_custom_call" | custom-call | flops 160432128 | bytes 638976 | tf_op jit(solution)/shard_map/match_next/pallas_call | solution.py:339
  29.2 0.2 collective-permute-done.9.refs_5_
  29.4 0.7 %match_next.3 = f32[8,1,128]{2,1,0:T(1,128)S(1)} custom-call(bf16[272,768]{1,0:T(8,128)(2,1)S(1)} %get-tuple-element.19.refs_0_, f32[272,128]{1,0:T(8,128)S(1)} %get-tuple-element.20.refs_1_, f32[272,128]{1,0:T(8,128)S(1)} %get-tuple-element.21.refs_2_, f32[272,128]{1,0:T(8,128)S(1)} %match_next.2.refs_3_, ...), custom_call_target="tpu_custom_call" | custom-call | flops 160432128 | bytes 638976 | tf_op jit(solution)/shard_map/match_next/pallas_call | solution.py:339
  30.1 10.2 %all_to_all.5.best_ref = f32[8,1,128]{2,1,0:T(1,128)S(1)} all-to-all(f32[8,1,128]{2,1,0:T(1,128)S(1)} %match_next.3), channel_id=1, replica_groups=mesh['z'=4,'core'=2,'y'=2,'x'=2] {'z','x'}, dimensions={0} | all-to-all | bytes 8192 | tf_op jit(solution)/shard_map/all_to_all | solution.py:407
  40.4 0.7 %collect.1 = f32[2,128]{1,0:T(2,128)} custom-call(s32[2,256]{1,0:T(2,128)S(1)} %get-tuple-element.14.info_ref, f32[8,1,128]{2,1,0:T(1,128)S(1)} %all_to_all.5.best_ref), custom_call_target="tpu_custom_call" | custom-call | tf_op jit(solution)/shard_map/collect/pallas_call | solution.py:370
  (20 shorter events, 0.3 us)
Async XLA Ops:
  1.5 6.1 %collective-permute-start = (bf16[2,208,128]{2,1,0:T(8,128)(2,1)S(1)}, bf16[2,208,128]{2,1,0:T(8,128)(2,1)S(1)}, u32[]{:S(2)}, u32[]{:S(2)}) collective-permute-start(bf16[2,208,128]{2,1,0:T(8,128)(2,1)S(1)} %get-tuple-element.16), channel_id=1, source_target_pairs={{0,8},{8,0},{16,24},{24,16},{1,9},{9,1},{17,25},{25,17},{2,10},{10... | collective-permute-start | bytes 319496 | tf_op jit(solution)/shard_map/ppermute | solution.py:381
  4.6 11.0 %collective-permute-start.2 = (bf16[2,208,128]{2,1,0:T(8,128)(2,1)S(1)}, bf16[2,208,128]{2,1,0:T(8,128)(2,1)S(1)}, u32[]{:S(2)}, u32[]{:S(2)}) collective-permute-start(bf16[2,208,128]{2,1,0:T(8,128)(2,1)S(1)} %get-tuple-element.17), channel_id=1, source_target_pairs={{0,16},{8,24},{16,0},{24,8},{1,17},{9,25},{17,1},{25,9},{2,18},{10... | collective-permute-start | bytes 319496 | tf_op jit(solution)/shard_map/ppermute | solution.py:381
  7.2 10.0 %collective-permute-start.4 = (bf16[2,208,128]{2,1,0:T(8,128)(2,1)S(1)}, bf16[2,208,128]{2,1,0:T(8,128)(2,1)S(1)}, u32[]{:S(2)}, u32[]{:S(2)}) collective-permute-start(bf16[2,208,128]{2,1,0:T(8,128)(2,1)S(1)} %get-tuple-element.18), channel_id=1, source_target_pairs={{0,24},{8,16},{16,8},{24,0},{1,25},{9,17},{17,9},{25,1},{2,26},{10... | collective-permute-start | bytes 319496 | tf_op jit(solution)/shard_map/ppermute | solution.py:381
  7.6 10.2 %collective-permute-start.1 = (bf16[2,208,128]{2,1,0:T(8,128)(2,1)S(1)}, bf16[2,208,128]{2,1,0:T(8,128)(2,1)S(1)}, u32[]{:S(2)}, u32[]{:S(2)}) collective-permute-start(bf16[2,208,128]{2,1,0:T(8,128)(2,1)S(1)} %pad_maximum_fusion.3), channel_id=1, source_target_pairs={{0,1},{1,0},{2,3},{3,2},{4,5},{5,4},{6,7},{7,6},{8,9},{9,8},{10,11... | collective-permute-start | bytes 319496 | tf_op jit(solution)/shard_map/ppermute | solution.py:381
  15.7 7.4 %collective-permute-start.3 = (bf16[1,208,128]{2,1,0:T(8,128)(2,1)S(1)}, bf16[1,208,128]{2,1,0:T(8,128)(2,1)S(1)}, u32[]{:S(2)}, u32[]{:S(2)}) collective-permute-start(bf16[1,208,128]{2,1,0:T(8,128)(2,1)S(1)} %get-tuple-element.34), channel_id=1, source_target_pairs={{0,1},{1,0},{2,3},{3,2},{4,5},{5,4},{6,7},{7,6},{8,9},{9,8},{10,11... | collective-permute-start | bytes 159752 | tf_op jit(solution)/shard_map/ppermute | solution.py:381
  17.3 4.2 %collective-permute-start.5 = (bf16[1,208,128]{2,1,0:T(8,128)(2,1)S(1)}, bf16[1,208,128]{2,1,0:T(8,128)(2,1)S(1)}, u32[]{:S(2)}, u32[]{:S(2)}) collective-permute-start(bf16[1,208,128]{2,1,0:T(8,128)(2,1)S(1)} %get-tuple-element.32), channel_id=1, source_target_pairs={{0,1},{1,0},{2,3},{3,2},{4,5},{5,4},{6,7},{7,6},{8,9},{9,8},{10,11... | collective-permute-start | bytes 159752 | tf_op jit(solution)/shard_map/ppermute | solution.py:381
  18.0 6.0 %collective-permute-start.6 = (bf16[4,208,128]{2,1,0:T(8,128)(2,1)S(1)}, bf16[4,208,128]{2,1,0:T(8,128)(2,1)S(1)}, u32[]{:S(2)}, u32[]{:S(2)}) collective-permute-start(bf16[4,208,128]{2,1,0:T(8,128)(2,1)S(1)} %pad_maximum_fusion.refs_0_), channel_id=1, source_target_pairs={{0,2},{2,0},{1,3},{3,1},{4,6},{6,4},{5,7},{7,5},{8,10},{10,8},{9,1... | collective-permute-start | bytes 638984 | tf_op jit(solution)/shard_map/ppermute | solution.py:381
  21.5 4.8 %collective-permute-start.10 = (bf16[2,208,128]{2,1,0:T(8,128)(2,1)S(1)}, bf16[2,208,128]{2,1,0:T(8,128)(2,1)S(1)}, u32[]{:S(2)}, u32[]{:S(2)}) collective-permute-start(bf16[2,208,128]{2,1,0:T(8,128)(2,1)S(1)} %pad_maximum_fusion.5.refs_2_), channel_id=1, source_target_pairs={{0,2},{2,0},{1,3},{3,1},{4,6},{6,4},{5,7},{7,5},{8,10},{10,8},{9,1... | collective-permute-start | bytes 319496 | tf_op jit(solution)/shard_map/ppermute | solution.py:381
  23.1 4.8 %collective-permute-start.8 = (bf16[2,208,128]{2,1,0:T(8,128)(2,1)S(1)}, bf16[2,208,128]{2,1,0:T(8,128)(2,1)S(1)}, u32[]{:S(2)}, u32[]{:S(2)}) collective-permute-start(bf16[2,208,128]{2,1,0:T(8,128)(2,1)S(1)} %pad_maximum_fusion.4.refs_1_), channel_id=1, source_target_pairs={{0,2},{2,0},{1,3},{3,1},{4,6},{6,4},{5,7},{7,5},{8,10},{10,8},{9,1... | collective-permute-start | bytes 319496 | tf_op jit(solution)/shard_map/ppermute | solution.py:381
  24.0 4.6 %collective-permute-start.7 = (bf16[8,208,128]{2,1,0:T(8,128)(2,1)S(1)}, bf16[8,208,128]{2,1,0:T(8,128)(2,1)S(1)}, u32[]{:S(2)}, u32[]{:S(2)}) collective-permute-start(bf16[8,208,128]{2,1,0:T(8,128)(2,1)S(1)} %constant_dynamic-update-slice_fusion), channel_id=1, source_target_pairs={{0,4},{4,0},{1,5},{5,1},{2,6},{6,2},{3,7},{7,3},{8,12},{12,8},{9,1... | collective-permute-start | bytes 1277960 | tf_op jit(solution)/shard_map/ppermute | solution.py:381
  26.3 2.9 %collective-permute-start.11 = (bf16[4,208,128]{2,1,0:T(8,128)(2,1)S(1)}, bf16[4,208,128]{2,1,0:T(8,128)(2,1)S(1)}, u32[]{:S(2)}, u32[]{:S(2)}) collective-permute-start(bf16[4,208,128]{2,1,0:T(8,128)(2,1)S(1)} %pad_maximum_fusion.2), channel_id=1, source_target_pairs={{0,4},{4,0},{1,5},{5,1},{2,6},{6,2},{3,7},{7,3},{8,12},{12,8},{9,1... | collective-permute-start | bytes 638984 | tf_op jit(solution)/shard_map/ppermute | solution.py:381
  27.9 1.5 %collective-permute-start.9 = (bf16[4,208,128]{2,1,0:T(8,128)(2,1)S(1)}, bf16[4,208,128]{2,1,0:T(8,128)(2,1)S(1)}, u32[]{:S(2)}, u32[]{:S(2)}) collective-permute-start(bf16[4,208,128]{2,1,0:T(8,128)(2,1)S(1)} %pad_maximum_fusion.1), channel_id=1, source_target_pairs={{0,4},{4,0},{1,5},{5,1},{2,6},{6,2},{3,7},{7,3},{8,12},{12,8},{9,1... | collective-permute-start | bytes 638984 | tf_op jit(solution)/shard_map/ppermute | solution.py:381

commit v3 on v2

--- a/solution.py
+++ b/solution.py
@@ -12,6 +12,7 @@
 TAIL = 16
 CLUSTER_DIGITS = 2
 RANK_DIGITS = 3
+FETCHES = 1
 VMEM_LIMIT = 48 * 1024 * 1024
 
 
@@ -81,15 +82,14 @@
 
 def place_kernel(s, layout, embed_hbm, cluster_hbm, rank_hbm, info_ref, *refs):
     out_refs, (embed_ref, cluster_ref, rank_ref, arrival) = refs[: len(layout)], refs[len(layout) :]
-    pairs = ((embed_hbm, embed_ref), (cluster_hbm, cluster_ref), (rank_hbm, rank_ref))
+    part = s.rows // FETCHES
+    pairs = [(cluster_hbm, cluster_ref), (rank_hbm, rank_ref)]
+    pairs += [(embed_hbm.at[pl.ds(i * part, part)], embed_ref.at[pl.ds(i * part, part)]) for i in range(FETCHES)]
     copies = [pltpu.make_async_copy(src, dst, arrival.at[i]) for i, (src, dst) in enumerate(pairs)]
     for copy in copies:
         copy.start()
-    for copy in copies:
+    for copy in copies[:2]:
         copy.wait()
-    widened = embed_ref[...].astype(jnp.float32)
-    total = jnp.sum(widened * widened, axis=1, keepdims=True)
-    unit = (widened * lax.rsqrt(total + 1e-06)).astype(jnp.bfloat16)
     cluster = row_of(cluster_ref)
     rank = row_of(rank_ref)
     n = s.classes
@@ -102,7 +102,6 @@
     within = jnp.sum(before * member, axis=0, keepdims=True).astype(jnp.int32)
     position = relative * s.stride + within
     placed = (iota((n * s.stride, s.rows), 0) == position).astype(jnp.float32).astype(jnp.bfloat16)
-    grouped = dot(placed, unit)
     local = (cluster >> shift) + 1
     digits = [(local >> (8 * i)) & 255 for i in range(CLUSTER_DIGITS)]
     digits += [(rank >> (8 * i)) & 255 for i in range(RANK_DIGITS)]
@@ -111,6 +110,12 @@
     for i, digit in enumerate(digits):
         fields = jnp.where(line == s.chunks + i, digit, fields)
     spread = dot(fields.astype(jnp.float32).astype(jnp.bfloat16), placed, ((1,), (1,)))
+    for copy in copies[2:]:
+        copy.wait()
+    widened = embed_ref[...].astype(jnp.float32)
+    total = jnp.sum(widened * widened, axis=1, keepdims=True)
+    unit = (widened * lax.rsqrt(total + 1e-06)).astype(jnp.bfloat16)
+    grouped = dot(placed, unit)
     tail_line = iota((TAIL, LANES), 0)
     for ref, members in zip(out_refs, layout):
         for slot, r in enumerate(members):
@@ -142,7 +147,7 @@
             pltpu.VMEM(embed.shape, embed.dtype),
             pltpu.VMEM((s.rows // LANES, LANES), jnp.int32),
             pltpu.VMEM((s.rows // LANES, LANES), jnp.int32),
-            pltpu.SemaphoreType.DMA((3,)),
+            pltpu.SemaphoreType.DMA((2 + FETCHES,)),
         ],
         compiler_params=pltpu.CompilerParams(vmem_limit_bytes=VMEM_LIMIT),
         name="place",
@@ -162,16 +167,20 @@
         tail_ref[b * TAIL : (b + 1) * TAIL, :] = ref[j, s.tail_at : s.block_rows, :]
 
 
+def split(value, by):
+    if by & (by - 1):
+        return value // by, value % by
+    return value >> (by.bit_length() - 1), value & (by - 1)
+
+
 def sorted_tails(s, tails, blocks, group):
     per = blocks // group
     padded = -(-per // 8) * 8
     used = s.chunks + CLUSTER_DIGITS + RANK_DIGITS
     lines = used * group * padded
     line = iota((lines, blocks * TAIL), 0)
-    r = line % padded
-    rest = line // padded
-    m = rest % group
-    field = rest // group
+    rest, r = split(line, padded)
+    field, m = split(rest, group)
     source = jnp.where(r < per, (r * group + m) * TAIL + field, -1)
     pick = (iota((lines, blocks * TAIL), 1) == source).astype(jnp.float32).astype(jnp.bfloat16)
     picked = dot(pick, tails)
@@ -395,8 +404,8 @@
         for a in queries:
             over = swap(a, "y", 1)
             waves.append([over, swap(jnp.concatenate([a, over]), "core", 1)])
-        state = match_next(s, order, state, waves[0], False)
-        state = match_next(s, order, state, [a for wave in waves[1:] for a in wave], True)
+        state = match_next(s, order, state, [wave[0] for wave in waves] + [waves[0][1]], False)
+        state = match_next(s, order, state, [wave[1] for wave in waves[1:]], True)
     else:
         everyone = lax.all_gather(jnp.concatenate(queries), ("core", "y"), axis=0)
         me = lax.axis_index(("core", "y"))

time: 41.2 us -> 41 us (level)
  waiting for transfers between devices: 12.8 us -> 10.2 us
  blocking collectives: 10.2 us -> 11.6 us
  starting transfers between devices: 13.5 us -> 14.5 us
    ppermute x12, waiting for transfers between devices: 12.8 us -> 10.2 us  [swap(): return lax.ppermute(array, axis, [(i, i ^ flip) for i in range(size)])]
    all_to_all x1, blocking collectives: 10.2 us -> 11.6 us  [local(): lax.all_to_all(state[3], ('z', 'x'), split_axis=0, concat_axis=0, tiled=T...]
    ppermute x12, starting transfers between devices: 13.5 us -> 14.5 us  [swap(): return lax.ppermute(array, axis, [(i, i ^ flip) for i in range(size)])]
where the time goes in v3:
time: 41 us; the launch traced here: 40.8 us
  starting transfers between devices  14.5 us (35%)
  blocking collectives  11.6 us (28%)
  waiting for transfers between devices  10.2 us (25%)
  Pallas kernels  4.08 us (10%)
    ppermute x12, starting transfers between devices, swap(): return lax.ppermute(array, axis, [(i, i ^ flip) for i in range(size)])  14.5 us
    all_to_all x1, blocking collectives, local(): lax.all_to_all(state[3], ('z', 'x'), split_axis=0, concat_axis=0, tiled=T...  11.6 us
    ppermute x12, waiting for transfers between devices, swap(): return lax.ppermute(array, axis, [(i, i ^ flip) for i in range(size)])  10.2 us
    pallas_call x1, Pallas kernels, place(): pl.pallas_call(functools.partial(place_kernel, s, layout), out_shape=outs...  1.53 us
    pallas_call x2, Pallas kernels, match_next(): pl.pallas_call(functools.partial(next_kernel, s, order, len(keys), last),...  1.24 us
  transfers between devices with their start and end apart: 12, of which 7 were waited for; matrix products, arithmetic and copies ran while one was open for 1% of the time, Pallas kernels for 3%

profile of v3, /device:TPU:0, one launch (start us, length us, event | category | flops | bytes accessed | tf_op | source)
XLA Modules:
  0.0 40.8 jit_solution(15442631148627693944)
XLA Ops:
  0.0 1.5 %place.1 = (s32[2,256]{1,0:T(2,128)S(1)}, bf16[2,208,128]{2,1,0:T(8,128)(2,1)S(1)}, bf16[2,208,128]{2,1,0:T(8,128)(2,1)S(1)}, bf16[2,208,128]{2,1,0:T(8,128)(2,1)S(1)}, bf16[2,208,128]{2,1,0:T(8,128)(2,1)S(1)}) custom-call(bf16[256,768]{1,0:T(8,128)(2,1)} %embed_hbm.1, s32[2,128]{1,0:T(2,128)} %bitcast.3, s32[2,128]{1,0:T(2,128)} %bitcast.4), custom_call_target="tpu_custom_call" | custom-call | tf_op jit(solution)/shard_map/place/pallas_call | solution.py:142
  1.5 3.1 %collective-permute-start = (bf16[2,208,128]{2,1,0:T(8,128)(2,1)S(1)}, bf16[2,208,128]{2,1,0:T(8,128)(2,1)S(1)}, u32[]{:S(2)}, u32[]{:S(2)}) collective-permute-start(bf16[2,208,128]{2,1,0:T(8,128)(2,1)S(1)} %get-tuple-element.16), channel_id=1, source_target_pairs={{0,8},{8,0},{16,24},{24,16},{1,9},{9,1},{17,25},{25,17},{2,10},{10... | collective-permute-start | bytes 319496 | tf_op jit(solution)/shard_map/ppermute | solution.py:390
  4.6 2.6 %collective-permute-start.2 = (bf16[2,208,128]{2,1,0:T(8,128)(2,1)S(1)}, bf16[2,208,128]{2,1,0:T(8,128)(2,1)S(1)}, u32[]{:S(2)}, u32[]{:S(2)}) collective-permute-start(bf16[2,208,128]{2,1,0:T(8,128)(2,1)S(1)} %get-tuple-element.17), channel_id=1, source_target_pairs={{0,16},{8,24},{16,0},{24,8},{1,17},{9,25},{17,1},{25,9},{2,18},{10... | collective-permute-start | bytes 319496 | tf_op jit(solution)/shard_map/ppermute | solution.py:390
  7.2 0.4 collective-permute-done
  7.6 1.7 %collective-permute-start.1 = (bf16[2,208,128]{2,1,0:T(8,128)(2,1)S(1)}, bf16[2,208,128]{2,1,0:T(8,128)(2,1)S(1)}, u32[]{:S(2)}, u32[]{:S(2)}) collective-permute-start(bf16[2,208,128]{2,1,0:T(8,128)(2,1)S(1)} %pad_maximum_fusion.3), channel_id=1, source_target_pairs={{0,1},{1,0},{2,3},{3,2},{4,5},{5,4},{6,7},{7,6},{8,9},{9,8},{10,11... | collective-permute-start | bytes 319496 | tf_op jit(solution)/shard_map/ppermute | solution.py:390
  9.4 6.3 %collective-permute-done.2 = bf16[2,208,128]{2,1,0:T(8,128)(2,1)S(1)} collective-permute-done((bf16[2,208,128]{2,1,0:T(8,128)(2,1)S(1)}, bf16[2,208,128]{2,1,0:T(8,128)(2,1)S(1)}, u32[]{:S(2)}, u32[]{:S(2)}) %collective-permute-start.2) | collective-permute-done | bytes 106528 | tf_op jit(solution)/shard_map/ppermute | solution.py:390
  15.7 1.6 %collective-permute-start.3 = (bf16[1,208,128]{2,1,0:T(8,128)(2,1)S(1)}, bf16[1,208,128]{2,1,0:T(8,128)(2,1)S(1)}, u32[]{:S(2)}, u32[]{:S(2)}) collective-permute-start(bf16[1,208,128]{2,1,0:T(8,128)(2,1)S(1)} %get-tuple-element.34), channel_id=1, source_target_pairs={{0,1},{1,0},{2,3},{3,2},{4,5},{5,4},{6,7},{7,6},{8,9},{9,8},{10,11... | collective-permute-start | bytes 159752 | tf_op jit(solution)/shard_map/ppermute | solution.py:390
  17.3 0.6 %collective-permute-start.5 = (bf16[1,208,128]{2,1,0:T(8,128)(2,1)S(1)}, bf16[1,208,128]{2,1,0:T(8,128)(2,1)S(1)}, u32[]{:S(2)}, u32[]{:S(2)}) collective-permute-start(bf16[1,208,128]{2,1,0:T(8,128)(2,1)S(1)} %get-tuple-element.32), channel_id=1, source_target_pairs={{0,1},{1,0},{2,3},{3,2},{4,5},{5,4},{6,7},{7,6},{8,9},{9,8},{10,11... | collective-permute-start | bytes 159752 | tf_op jit(solution)/shard_map/ppermute | solution.py:390
  18.0 1.6 %collective-permute-start.6 = (bf16[4,208,128]{2,1,0:T(8,128)(2,1)S(1)}, bf16[4,208,128]{2,1,0:T(8,128)(2,1)S(1)}, u32[]{:S(2)}, u32[]{:S(2)}) collective-permute-start(bf16[4,208,128]{2,1,0:T(8,128)(2,1)S(1)} %pad_maximum_fusion.refs_0_), channel_id=1, source_target_pairs={{0,2},{2,0},{1,3},{3,1},{4,6},{6,4},{5,7},{7,5},{8,10},{10,8},{9,1... | collective-permute-start | bytes 638984 | tf_op jit(solution)/shard_map/ppermute | solution.py:390
  19.6 0.3 collective-permute-done.3
  19.9 1.6 %collective-permute-start.7 = (bf16[2,208,128]{2,1,0:T(8,128)(2,1)S(1)}, bf16[2,208,128]{2,1,0:T(8,128)(2,1)S(1)}, u32[]{:S(2)}, u32[]{:S(2)}) collective-permute-start(bf16[2,208,128]{2,1,0:T(8,128)(2,1)S(1)} %pad_maximum_fusion.4.refs_1_), channel_id=1, source_target_pairs={{0,2},{2,0},{1,3},{3,1},{4,6},{6,4},{5,7},{7,5},{8,10},{10,8},{9,1... | collective-permute-start | bytes 319496 | tf_op jit(solution)/shard_map/ppermute | solution.py:390
  21.5 1.6 %collective-permute-start.8 = (bf16[2,208,128]{2,1,0:T(8,128)(2,1)S(1)}, bf16[2,208,128]{2,1,0:T(8,128)(2,1)S(1)}, u32[]{:S(2)}, u32[]{:S(2)}) collective-permute-start(bf16[2,208,128]{2,1,0:T(8,128)(2,1)S(1)} %pad_maximum_fusion.5.refs_2_), channel_id=1, source_target_pairs={{0,2},{2,0},{1,3},{3,1},{4,6},{6,4},{5,7},{7,5},{8,10},{10,8},{9,1... | collective-permute-start | bytes 319496 | tf_op jit(solution)/shard_map/ppermute | solution.py:390
  23.1 0.9 %collective-permute-done.6.refs_4_ = bf16[4,208,128]{2,1,0:T(8,128)(2,1)S(1)} collective-permute-done((bf16[4,208,128]{2,1,0:T(8,128)(2,1)S(1)}, bf16[4,208,128]{2,1,0:T(8,128)(2,1)S(1)}, u32[]{:S(2)}, u32[]{:S(2)}) %collective-permute-start.6) | collective-permute-done | bytes 213024 | tf_op jit(solution)/shard_map/ppermute | solution.py:390
  24.0 0.1 collective-permute-start.9
  24.0 1.0 %collective-permute-done.7.refs_5_ = bf16[2,208,128]{2,1,0:T(8,128)(2,1)S(1)} collective-permute-done((bf16[2,208,128]{2,1,0:T(8,128)(2,1)S(1)}, bf16[2,208,128]{2,1,0:T(8,128)(2,1)S(1)}, u32[]{:S(2)}, u32[]{:S(2)}) %collective-permute-start.7) | collective-permute-done | bytes 106528 | tf_op jit(solution)/shard_map/ppermute | solution.py:390
  25.1 0.1 collective-permute-start.10
  25.2 1.1 %collective-permute-done.8.refs_6_ = bf16[2,208,128]{2,1,0:T(8,128)(2,1)S(1)} collective-permute-done((bf16[2,208,128]{2,1,0:T(8,128)(2,1)S(1)}, bf16[2,208,128]{2,1,0:T(8,128)(2,1)S(1)}, u32[]{:S(2)}, u32[]{:S(2)}) %collective-permute-start.8) | collective-permute-done | bytes 106528 | tf_op jit(solution)/shard_map/ppermute | solution.py:390
  26.3 0.1 collective-permute-start.11
  26.4 0.6 %match_first.1 = (bf16[272,768]{1,0:T(8,128)(2,1)S(1)}, f32[272,128]{1,0:T(8,128)S(1)}, f32[272,128]{1,0:T(8,128)S(1)}, f32[272,128]{1,0:T(8,128)S(1)}) custom-call(bf16[4,208,128]{2,1,0:T(8,128)(2,1)S(1)} %pad_maximum_fusion.refs_0_, bf16[2,208,128]{2,1,0:T(8,128)(2,1)S(1)} %pad_maximum_fusion.4.refs_1_, bf16[2,208,128]{2,1,0:T(8,128)(2,1)S(1)} %pad_maximum_fusion.5.refs_2_), custom_call_target="tpu_custom_call" | custom-call | flops 106954752 | bytes 425984 | tf_op jit(solution)/shard_map/match_first/pallas_call | solution.py:330
  27.0 0.6 %match_next.2.refs_3_ = f32[272,128]{1,0:T(8,128)S(1)} custom-call(bf16[272,768]{1,0:T(8,128)(2,1)S(1)} %get-tuple-element.19.refs_0_, f32[272,128]{1,0:T(8,128)S(1)} %get-tuple-element.20.refs_1_, f32[272,128]{1,0:T(8,128)S(1)} %get-tuple-element.21.refs_2_, f32[272,128]{1,0:T(8,128)S(1)} %get-tuple-element.22.refs_3_, ...), custom_call_target="tpu_custom_call" | custom-call | flops 213909504 | bytes 851968 | tf_op jit(solution)/shard_map/match_next/pallas_call | solution.py:348
  27.6 0.2 collective-permute-done.11.refs_5_
  27.8 0.6 %match_next.3 = f32[8,1,128]{2,1,0:T(1,128)S(1)} custom-call(bf16[272,768]{1,0:T(8,128)(2,1)S(1)} %get-tuple-element.19.refs_0_, f32[272,128]{1,0:T(8,128)S(1)} %get-tuple-element.20.refs_1_, f32[272,128]{1,0:T(8,128)S(1)} %get-tuple-element.21.refs_2_, f32[272,128]{1,0:T(8,128)S(1)} %match_next.2.refs_3_, ...), custom_call_target="tpu_custom_call" | custom-call | flops 106954752 | bytes 425984 | tf_op jit(solution)/shard_map/match_next/pallas_call | solution.py:348
  28.5 11.6 %all_to_all.5.best_ref = f32[8,1,128]{2,1,0:T(1,128)S(1)} all-to-all(f32[8,1,128]{2,1,0:T(1,128)S(1)} %match_next.3), channel_id=1, replica_groups=mesh['z'=4,'core'=2,'y'=2,'x'=2] {'z','x'}, dimensions={0} | all-to-all | bytes 8192 | tf_op jit(solution)/shard_map/all_to_all | solution.py:416
  40.1 0.7 %collect.1 = f32[2,128]{1,0:T(2,128)} custom-call(s32[2,256]{1,0:T(2,128)S(1)} %get-tuple-element.14.info_ref, f32[8,1,128]{2,1,0:T(1,128)S(1)} %all_to_all.5.best_ref), custom_call_target="tpu_custom_call" | custom-call | tf_op jit(solution)/shard_map/collect/pallas_call | solution.py:379
  (20 shorter events, 0.3 us)
Async XLA Ops:
  1.5 6.1 %collective-permute-start = (bf16[2,208,128]{2,1,0:T(8,128)(2,1)S(1)}, bf16[2,208,128]{2,1,0:T(8,128)(2,1)S(1)}, u32[]{:S(2)}, u32[]{:S(2)}) collective-permute-start(bf16[2,208,128]{2,1,0:T(8,128)(2,1)S(1)} %get-tuple-element.16), channel_id=1, source_target_pairs={{0,8},{8,0},{16,24},{24,16},{1,9},{9,1},{17,25},{25,17},{2,10},{10... | collective-permute-start | bytes 319496 | tf_op jit(solution)/shard_map/ppermute | solution.py:390
  4.6 11.0 %collective-permute-start.2 = (bf16[2,208,128]{2,1,0:T(8,128)(2,1)S(1)}, bf16[2,208,128]{2,1,0:T(8,128)(2,1)S(1)}, u32[]{:S(2)}, u32[]{:S(2)}) collective-permute-start(bf16[2,208,128]{2,1,0:T(8,128)(2,1)S(1)} %get-tuple-element.17), channel_id=1, source_target_pairs={{0,16},{8,24},{16,0},{24,8},{1,17},{9,25},{17,1},{25,9},{2,18},{10... | collective-permute-start | bytes 319496 | tf_op jit(solution)/shard_map/ppermute | solution.py:390
  7.2 10.0 %collective-permute-start.4 = (bf16[2,208,128]{2,1,0:T(8,128)(2,1)S(1)}, bf16[2,208,128]{2,1,0:T(8,128)(2,1)S(1)}, u32[]{:S(2)}, u32[]{:S(2)}) collective-permute-start(bf16[2,208,128]{2,1,0:T(8,128)(2,1)S(1)} %get-tuple-element.18), channel_id=1, source_target_pairs={{0,24},{8,16},{16,8},{24,0},{1,25},{9,17},{17,9},{25,1},{2,26},{10... | collective-permute-start | bytes 319496 | tf_op jit(solution)/shard_map/ppermute | solution.py:390
  7.6 10.2 %collective-permute-start.1 = (bf16[2,208,128]{2,1,0:T(8,128)(2,1)S(1)}, bf16[2,208,128]{2,1,0:T(8,128)(2,1)S(1)}, u32[]{:S(2)}, u32[]{:S(2)}) collective-permute-start(bf16[2,208,128]{2,1,0:T(8,128)(2,1)S(1)} %pad_maximum_fusion.3), channel_id=1, source_target_pairs={{0,1},{1,0},{2,3},{3,2},{4,5},{5,4},{6,7},{7,6},{8,9},{9,8},{10,11... | collective-permute-start | bytes 319496 | tf_op jit(solution)/shard_map/ppermute | solution.py:390
  15.7 4.2 %collective-permute-start.3 = (bf16[1,208,128]{2,1,0:T(8,128)(2,1)S(1)}, bf16[1,208,128]{2,1,0:T(8,128)(2,1)S(1)}, u32[]{:S(2)}, u32[]{:S(2)}) collective-permute-start(bf16[1,208,128]{2,1,0:T(8,128)(2,1)S(1)} %get-tuple-element.34), channel_id=1, source_target_pairs={{0,1},{1,0},{2,3},{3,2},{4,5},{5,4},{6,7},{7,6},{8,9},{9,8},{10,11... | collective-permute-start | bytes 159752 | tf_op jit(solution)/shard_map/ppermute | solution.py:390
  17.3 4.2 %collective-permute-start.5 = (bf16[1,208,128]{2,1,0:T(8,128)(2,1)S(1)}, bf16[1,208,128]{2,1,0:T(8,128)(2,1)S(1)}, u32[]{:S(2)}, u32[]{:S(2)}) collective-permute-start(bf16[1,208,128]{2,1,0:T(8,128)(2,1)S(1)} %get-tuple-element.32), channel_id=1, source_target_pairs={{0,1},{1,0},{2,3},{3,2},{4,5},{5,4},{6,7},{7,6},{8,9},{9,8},{10,11... | collective-permute-start | bytes 159752 | tf_op jit(solution)/shard_map/ppermute | solution.py:390
  18.0 6.0 %collective-permute-start.6 = (bf16[4,208,128]{2,1,0:T(8,128)(2,1)S(1)}, bf16[4,208,128]{2,1,0:T(8,128)(2,1)S(1)}, u32[]{:S(2)}, u32[]{:S(2)}) collective-permute-start(bf16[4,208,128]{2,1,0:T(8,128)(2,1)S(1)} %pad_maximum_fusion.refs_0_), channel_id=1, source_target_pairs={{0,2},{2,0},{1,3},{3,1},{4,6},{6,4},{5,7},{7,5},{8,10},{10,8},{9,1... | collective-permute-start | bytes 638984 | tf_op jit(solution)/shard_map/ppermute | solution.py:390
  19.9 5.2 %collective-permute-start.7 = (bf16[2,208,128]{2,1,0:T(8,128)(2,1)S(1)}, bf16[2,208,128]{2,1,0:T(8,128)(2,1)S(1)}, u32[]{:S(2)}, u32[]{:S(2)}) collective-permute-start(bf16[2,208,128]{2,1,0:T(8,128)(2,1)S(1)} %pad_maximum_fusion.4.refs_1_), channel_id=1, source_target_pairs={{0,2},{2,0},{1,3},{3,1},{4,6},{6,4},{5,7},{7,5},{8,10},{10,8},{9,1... | collective-permute-start | bytes 319496 | tf_op jit(solution)/shard_map/ppermute | solution.py:390
  21.5 4.8 %collective-permute-start.8 = (bf16[2,208,128]{2,1,0:T(8,128)(2,1)S(1)}, bf16[2,208,128]{2,1,0:T(8,128)(2,1)S(1)}, u32[]{:S(2)}, u32[]{:S(2)}) collective-permute-start(bf16[2,208,128]{2,1,0:T(8,128)(2,1)S(1)} %pad_maximum_fusion.5.refs_2_), channel_id=1, source_target_pairs={{0,2},{2,0},{1,3},{3,1},{4,6},{6,4},{5,7},{7,5},{8,10},{10,8},{9,1... | collective-permute-start | bytes 319496 | tf_op jit(solution)/shard_map/ppermute | solution.py:390
  24.0 3.0 %collective-permute-start.9 = (bf16[8,208,128]{2,1,0:T(8,128)(2,1)S(1)}, bf16[8,208,128]{2,1,0:T(8,128)(2,1)S(1)}, u32[]{:S(2)}, u32[]{:S(2)}) collective-permute-start(bf16[8,208,128]{2,1,0:T(8,128)(2,1)S(1)} %constant_dynamic-update-slice_fusion), channel_id=1, source_target_pairs={{0,4},{4,0},{1,5},{5,1},{2,6},{6,2},{3,7},{7,3},{8,12},{12,8},{9,1... | collective-permute-start | bytes 1277960 | tf_op jit(solution)/shard_map/ppermute | solution.py:390
  25.1 2.5 %collective-permute-start.10 = (bf16[4,208,128]{2,1,0:T(8,128)(2,1)S(1)}, bf16[4,208,128]{2,1,0:T(8,128)(2,1)S(1)}, u32[]{:S(2)}, u32[]{:S(2)}) collective-permute-start(bf16[4,208,128]{2,1,0:T(8,128)(2,1)S(1)} %pad_maximum_fusion.1), channel_id=1, source_target_pairs={{0,4},{4,0},{1,5},{5,1},{2,6},{6,2},{3,7},{7,3},{8,12},{12,8},{9,1... | collective-permute-start | bytes 638984 | tf_op jit(solution)/shard_map/ppermute | solution.py:390
  26.3 1.5 %collective-permute-start.11 = (bf16[4,208,128]{2,1,0:T(8,128)(2,1)S(1)}, bf16[4,208,128]{2,1,0:T(8,128)(2,1)S(1)}, u32[]{:S(2)}, u32[]{:S(2)}) collective-permute-start(bf16[4,208,128]{2,1,0:T(8,128)(2,1)S(1)} %pad_maximum_fusion.2), channel_id=1, source_target_pairs={{0,4},{4,0},{1,5},{5,1},{2,6},{6,2},{3,7},{7,3},{8,12},{12,8},{9,1... | collective-permute-start | bytes 638984 | tf_op jit(solution)/shard_map/ppermute | solution.py:390

commit v4 on v3

--- a/solution.py
+++ b/solution.py
@@ -9,7 +9,9 @@
 from jax.sharding import Mesh, PartitionSpec as P
 
 LANES = 128
-TAIL = 16
+TAIL = 8
+FIELD_LINES = 16
+PER_LINE = 3
 CLUSTER_DIGITS = 2
 RANK_DIGITS = 3
 FETCHES = 1
@@ -105,10 +107,10 @@
     local = (cluster >> shift) + 1
     digits = [(local >> (8 * i)) & 255 for i in range(CLUSTER_DIGITS)]
     digits += [(rank >> (8 * i)) & 255 for i in range(RANK_DIGITS)]
-    line = iota((TAIL, s.rows), 0)
-    fields = jnp.zeros((TAIL, s.rows), jnp.int32)
+    line = iota((FIELD_LINES, s.rows), 0)
+    fields = jnp.zeros((FIELD_LINES, s.rows), jnp.int32)
     for i, digit in enumerate(digits):
-        fields = jnp.where(line == s.chunks + i, digit, fields)
+        fields = jnp.where(line == i, digit, fields)
     spread = dot(fields.astype(jnp.float32).astype(jnp.bfloat16), placed, ((1,), (1,)))
     for copy in copies[2:]:
         copy.wait()
@@ -124,9 +126,13 @@
                 ref[slot, c * s.base : (c + 1) * s.base, :] = grouped[
                     at : at + s.base, c * LANES : (c + 1) * LANES
                 ].astype(jnp.bfloat16)
-            tail = jnp.concatenate(
-                [spread[:, at : at + s.stride], jnp.zeros((TAIL, LANES - s.stride), jnp.float32)], axis=1
-            )
+            tail = jnp.zeros((TAIL, LANES), jnp.float32)
+            for i in range(0, len(digits), PER_LINE):
+                parts = [spread[f : f + 1, at : at + s.stride] for f in range(i, i + PER_LINE)]
+                parts.append(jnp.zeros((1, LANES - PER_LINE * s.stride), jnp.float32))
+                tail = jnp.where(
+                    tail_line == s.chunks + i // PER_LINE, jnp.concatenate(parts, axis=1), tail
+                )
             if s.extra:
                 for c in range(s.chunks):
                     piece = grouped[at + s.base : at + s.base + 1, c * LANES : (c + 1) * LANES]
@@ -176,7 +182,7 @@
 def sorted_tails(s, tails, blocks, group):
     per = blocks // group
     padded = -(-per // 8) * 8
-    used = s.chunks + CLUSTER_DIGITS + RANK_DIGITS
+    used = s.chunks - (-(CLUSTER_DIGITS + RANK_DIGITS) // PER_LINE)
     lines = used * group * padded
     line = iota((lines, blocks * TAIL), 0)
     rest, r = split(line, padded)
@@ -186,10 +192,13 @@
     picked = dot(pick, tails)
     step = group * padded
     parts = [picked[f * step : (f + 1) * step] for f in range(used)]
-    at = s.chunks
-    cluster = parts[at] + 256.0 * parts[at + 1]
-    at += CLUSTER_DIGITS
-    rank = parts[at] + 256.0 * parts[at + 1] + 65536.0 * parts[at + 2]
+    digits = []
+    for i in range(CLUSTER_DIGITS + RANK_DIGITS):
+        digit = parts[s.chunks + i // PER_LINE]
+        lane = i % PER_LINE * s.stride
+        digits.append(pltpu.roll(digit, LANES - lane, 1) if lane else digit)
+    cluster = digits[0] + 256.0 * digits[1]
+    rank = digits[2] + 256.0 * digits[3] + 65536.0 * digits[4]
     return parts[: s.chunks], cluster, rank, padded
 
 

time: 41 us -> 40.1 us (0.978)
  blocking collectives: 11.6 us -> 11 us
    all_to_all x1, blocking collectives: 11.6 us -> 11 us  [local(): lax.all_to_all(state[3], ('z', 'x'), split_axis=0, concat_axis=0, tiled=T...]
where the time goes in v4:
time: 40.1 us; the launch traced here: 39.9 us
  starting transfers between devices  14.5 us (36%)
  blocking collectives  11 us (27%)
  waiting for transfers between devices  10 us (25%)
  Pallas kernels  4.04 us (10%)
    ppermute x12, starting transfers between devices, swap(): return lax.ppermute(array, axis, [(i, i ^ flip) for i in range(size)])  14.5 us
    all_to_all x1, blocking collectives, local(): lax.all_to_all(state[3], ('z', 'x'), split_axis=0, concat_axis=0, tiled=T...  11 us
    ppermute x12, waiting for transfers between devices, swap(): return lax.ppermute(array, axis, [(i, i ^ flip) for i in range(size)])  10 us
    pallas_call x1, Pallas kernels, place(): pl.pallas_call(functools.partial(place_kernel, s, layout), out_shape=outs...  1.53 us
    pallas_call x2, Pallas kernels, match_next(): pl.pallas_call(functools.partial(next_kernel, s, order, len(keys), last),...  1.21 us
  transfers between devices with their start and end apart: 12, of which 7 were waited for; matrix products, arithmetic and copies ran while one was open for 1% of the time, Pallas kernels for 3%

profile of v4, /device:TPU:0, one launch (start us, length us, event | category | flops | bytes accessed | tf_op | source)
XLA Modules:
  0.0 39.9 jit_solution(12584779604968961395)
XLA Ops:
  0.0 1.5 %place.1 = (s32[2,256]{1,0:T(2,128)S(1)}, bf16[2,200,128]{2,1,0:T(8,128)(2,1)S(1)}, bf16[2,200,128]{2,1,0:T(8,128)(2,1)S(1)}, bf16[2,200,128]{2,1,0:T(8,128)(2,1)S(1)}, bf16[2,200,128]{2,1,0:T(8,128)(2,1)S(1)}) custom-call(bf16[256,768]{1,0:T(8,128)(2,1)} %embed_hbm.1, s32[2,128]{1,0:T(2,128)} %bitcast.3, s32[2,128]{1,0:T(2,128)} %bitcast.4), custom_call_target="tpu_custom_call" | custom-call | tf_op jit(solution)/shard_map/place/pallas_call | solution.py:148
  1.5 3.1 %collective-permute-start = (bf16[2,200,128]{2,1,0:T(8,128)(2,1)S(1)}, bf16[2,200,128]{2,1,0:T(8,128)(2,1)S(1)}, u32[]{:S(2)}, u32[]{:S(2)}) collective-permute-start(bf16[2,200,128]{2,1,0:T(8,128)(2,1)S(1)} %get-tuple-element.16), channel_id=1, source_target_pairs={{0,8},{8,0},{16,24},{24,16},{1,9},{9,1},{17,25},{25,17},{2,10},{10... | collective-permute-start | bytes 307208 | tf_op jit(solution)/shard_map/ppermute | solution.py:399
  4.6 2.6 %collective-permute-start.2 = (bf16[2,200,128]{2,1,0:T(8,128)(2,1)S(1)}, bf16[2,200,128]{2,1,0:T(8,128)(2,1)S(1)}, u32[]{:S(2)}, u32[]{:S(2)}) collective-permute-start(bf16[2,200,128]{2,1,0:T(8,128)(2,1)S(1)} %get-tuple-element.17), channel_id=1, source_target_pairs={{0,16},{8,24},{16,0},{24,8},{1,17},{9,25},{17,1},{25,9},{2,18},{10... | collective-permute-start | bytes 307208 | tf_op jit(solution)/shard_map/ppermute | solution.py:399
  7.2 0.3 collective-permute-done
  7.5 1.8 %collective-permute-start.1 = (bf16[2,200,128]{2,1,0:T(8,128)(2,1)S(1)}, bf16[2,200,128]{2,1,0:T(8,128)(2,1)S(1)}, u32[]{:S(2)}, u32[]{:S(2)}) collective-permute-start(bf16[2,200,128]{2,1,0:T(8,128)(2,1)S(1)} %pad_maximum_fusion.3), channel_id=1, source_target_pairs={{0,1},{1,0},{2,3},{3,2},{4,5},{5,4},{6,7},{7,6},{8,9},{9,8},{10,11... | collective-permute-start | bytes 307208 | tf_op jit(solution)/shard_map/ppermute | solution.py:399
  9.3 6.1 %collective-permute-done.2 = bf16[2,200,128]{2,1,0:T(8,128)(2,1)S(1)} collective-permute-done((bf16[2,200,128]{2,1,0:T(8,128)(2,1)S(1)}, bf16[2,200,128]{2,1,0:T(8,128)(2,1)S(1)}, u32[]{:S(2)}, u32[]{:S(2)}) %collective-permute-start.2) | collective-permute-done | bytes 102432 | tf_op jit(solution)/shard_map/ppermute | solution.py:399
  15.4 1.6 %collective-permute-start.3 = (bf16[1,200,128]{2,1,0:T(8,128)(2,1)S(1)}, bf16[1,200,128]{2,1,0:T(8,128)(2,1)S(1)}, u32[]{:S(2)}, u32[]{:S(2)}) collective-permute-start(bf16[1,200,128]{2,1,0:T(8,128)(2,1)S(1)} %get-tuple-element.34), channel_id=1, source_target_pairs={{0,1},{1,0},{2,3},{3,2},{4,5},{5,4},{6,7},{7,6},{8,9},{9,8},{10,11... | collective-permute-start | bytes 153608 | tf_op jit(solution)/shard_map/ppermute | solution.py:399
  16.9 0.6 %collective-permute-start.5 = (bf16[1,200,128]{2,1,0:T(8,128)(2,1)S(1)}, bf16[1,200,128]{2,1,0:T(8,128)(2,1)S(1)}, u32[]{:S(2)}, u32[]{:S(2)}) collective-permute-start(bf16[1,200,128]{2,1,0:T(8,128)(2,1)S(1)} %get-tuple-element.32), channel_id=1, source_target_pairs={{0,1},{1,0},{2,3},{3,2},{4,5},{5,4},{6,7},{7,6},{8,9},{9,8},{10,11... | collective-permute-start | bytes 153608 | tf_op jit(solution)/shard_map/ppermute | solution.py:399
  17.7 1.6 %collective-permute-start.6 = (bf16[4,200,128]{2,1,0:T(8,128)(2,1)S(1)}, bf16[4,200,128]{2,1,0:T(8,128)(2,1)S(1)}, u32[]{:S(2)}, u32[]{:S(2)}) collective-permute-start(bf16[4,200,128]{2,1,0:T(8,128)(2,1)S(1)} %pad_maximum_fusion.refs_0_), channel_id=1, source_target_pairs={{0,2},{2,0},{1,3},{3,1},{4,6},{6,4},{5,7},{7,5},{8,10},{10,8},{9,1... | collective-permute-start | bytes 614408 | tf_op jit(solution)/shard_map/ppermute | solution.py:399
  19.2 0.3 collective-permute-done.3
  19.6 1.6 %collective-permute-start.7 = (bf16[2,200,128]{2,1,0:T(8,128)(2,1)S(1)}, bf16[2,200,128]{2,1,0:T(8,128)(2,1)S(1)}, u32[]{:S(2)}, u32[]{:S(2)}) collective-permute-start(bf16[2,200,128]{2,1,0:T(8,128)(2,1)S(1)} %pad_maximum_fusion.4.refs_1_), channel_id=1, source_target_pairs={{0,2},{2,0},{1,3},{3,1},{4,6},{6,4},{5,7},{7,5},{8,10},{10,8},{9,1... | collective-permute-start | bytes 307208 | tf_op jit(solution)/shard_map/ppermute | solution.py:399
  21.2 1.6 %collective-permute-start.8 = (bf16[2,200,128]{2,1,0:T(8,128)(2,1)S(1)}, bf16[2,200,128]{2,1,0:T(8,128)(2,1)S(1)}, u32[]{:S(2)}, u32[]{:S(2)}) collective-permute-start(bf16[2,200,128]{2,1,0:T(8,128)(2,1)S(1)} %pad_maximum_fusion.5.refs_2_), channel_id=1, source_target_pairs={{0,2},{2,0},{1,3},{3,1},{4,6},{6,4},{5,7},{7,5},{8,10},{10,8},{9,1... | collective-permute-start | bytes 307208 | tf_op jit(solution)/shard_map/ppermute | solution.py:399
  22.7 1.2 %collective-permute-done.6.refs_4_ = bf16[4,200,128]{2,1,0:T(8,128)(2,1)S(1)} collective-permute-done((bf16[4,200,128]{2,1,0:T(8,128)(2,1)S(1)}, bf16[4,200,128]{2,1,0:T(8,128)(2,1)S(1)}, u32[]{:S(2)}, u32[]{:S(2)}) %collective-permute-start.6) | collective-permute-done | bytes 204832 | tf_op jit(solution)/shard_map/ppermute | solution.py:399
  23.9 0.1 collective-permute-start.9
  24.0 1.0 %collective-permute-done.7.refs_5_ = bf16[2,200,128]{2,1,0:T(8,128)(2,1)S(1)} collective-permute-done((bf16[2,200,128]{2,1,0:T(8,128)(2,1)S(1)}, bf16[2,200,128]{2,1,0:T(8,128)(2,1)S(1)}, u32[]{:S(2)}, u32[]{:S(2)}) %collective-permute-start.7) | collective-permute-done | bytes 102432 | tf_op jit(solution)/shard_map/ppermute | solution.py:399
  25.0 0.1 collective-permute-start.10
  25.1 1.0 %collective-permute-done.8.refs_6_ = bf16[2,200,128]{2,1,0:T(8,128)(2,1)S(1)} collective-permute-done((bf16[2,200,128]{2,1,0:T(8,128)(2,1)S(1)}, bf16[2,200,128]{2,1,0:T(8,128)(2,1)S(1)}, u32[]{:S(2)}, u32[]{:S(2)}) %collective-permute-start.8) | collective-permute-done | bytes 102432 | tf_op jit(solution)/shard_map/ppermute | solution.py:399
  26.1 0.1 collective-permute-start.11
  26.2 0.6 %match_first.1 = (bf16[272,768]{1,0:T(8,128)(2,1)S(1)}, f32[272,128]{1,0:T(8,128)S(1)}, f32[272,128]{1,0:T(8,128)S(1)}, f32[272,128]{1,0:T(8,128)S(1)}) custom-call(bf16[4,200,128]{2,1,0:T(8,128)(2,1)S(1)} %pad_maximum_fusion.refs_0_, bf16[2,200,128]{2,1,0:T(8,128)(2,1)S(1)} %pad_maximum_fusion.4.refs_1_, bf16[2,200,128]{2,1,0:T(8,128)(2,1)S(1)} %pad_maximum_fusion.5.refs_2_), custom_call_target="tpu_custom_call" | custom-call | flops 106954752 | bytes 409600 | tf_op jit(solution)/shard_map/match_first/pallas_call | solution.py:339
  26.8 0.6 %match_next.2.refs_3_ = f32[272,128]{1,0:T(8,128)S(1)} custom-call(bf16[272,768]{1,0:T(8,128)(2,1)S(1)} %get-tuple-element.19.refs_0_, f32[272,128]{1,0:T(8,128)S(1)} %get-tuple-element.20.refs_1_, f32[272,128]{1,0:T(8,128)S(1)} %get-tuple-element.21.refs_2_, f32[272,128]{1,0:T(8,128)S(1)} %get-tuple-element.22.refs_3_, ...), custom_call_target="tpu_custom_call" | custom-call | flops 213909504 | bytes 819200 | tf_op jit(solution)/shard_map/match_next/pallas_call | solution.py:357
  27.4 0.2 collective-permute-done.11.refs_5_
  27.6 0.6 %match_next.3 = f32[8,1,128]{2,1,0:T(1,128)S(1)} custom-call(bf16[272,768]{1,0:T(8,128)(2,1)S(1)} %get-tuple-element.19.refs_0_, f32[272,128]{1,0:T(8,128)S(1)} %get-tuple-element.20.refs_1_, f32[272,128]{1,0:T(8,128)S(1)} %get-tuple-element.21.refs_2_, f32[272,128]{1,0:T(8,128)S(1)} %match_next.2.refs_3_, ...), custom_call_target="tpu_custom_call" | custom-call | flops 106954752 | bytes 409600 | tf_op jit(solution)/shard_map/match_next/pallas_call | solution.py:357
  28.3 11.0 %all_to_all.5.best_ref = f32[8,1,128]{2,1,0:T(1,128)S(1)} all-to-all(f32[8,1,128]{2,1,0:T(1,128)S(1)} %match_next.3), channel_id=1, replica_groups=mesh['z'=4,'core'=2,'y'=2,'x'=2] {'z','x'}, dimensions={0} | all-to-all | bytes 8192 | tf_op jit(solution)/shard_map/all_to_all | solution.py:425
  39.2 0.7 %collect.1 = f32[2,128]{1,0:T(2,128)} custom-call(s32[2,256]{1,0:T(2,128)S(1)} %get-tuple-element.14.info_ref, f32[8,1,128]{2,1,0:T(1,128)S(1)} %all_to_all.5.best_ref), custom_call_target="tpu_custom_call" | custom-call | tf_op jit(solution)/shard_map/collect/pallas_call | solution.py:388
  (20 shorter events, 0.2 us)
Async XLA Ops:
  1.5 6.0 %collective-permute-start = (bf16[2,200,128]{2,1,0:T(8,128)(2,1)S(1)}, bf16[2,200,128]{2,1,0:T(8,128)(2,1)S(1)}, u32[]{:S(2)}, u32[]{:S(2)}) collective-permute-start(bf16[2,200,128]{2,1,0:T(8,128)(2,1)S(1)} %get-tuple-element.16), channel_id=1, source_target_pairs={{0,8},{8,0},{16,24},{24,16},{1,9},{9,1},{17,25},{25,17},{2,10},{10... | collective-permute-start | bytes 307208 | tf_op jit(solution)/shard_map/ppermute | solution.py:399
  4.6 10.7 %collective-permute-start.2 = (bf16[2,200,128]{2,1,0:T(8,128)(2,1)S(1)}, bf16[2,200,128]{2,1,0:T(8,128)(2,1)S(1)}, u32[]{:S(2)}, u32[]{:S(2)}) collective-permute-start(bf16[2,200,128]{2,1,0:T(8,128)(2,1)S(1)} %get-tuple-element.17), channel_id=1, source_target_pairs={{0,16},{8,24},{16,0},{24,8},{1,17},{9,25},{17,1},{25,9},{2,18},{10... | collective-permute-start | bytes 307208 | tf_op jit(solution)/shard_map/ppermute | solution.py:399
  7.2 9.7 %collective-permute-start.4 = (bf16[2,200,128]{2,1,0:T(8,128)(2,1)S(1)}, bf16[2,200,128]{2,1,0:T(8,128)(2,1)S(1)}, u32[]{:S(2)}, u32[]{:S(2)}) collective-permute-start(bf16[2,200,128]{2,1,0:T(8,128)(2,1)S(1)} %get-tuple-element.18), channel_id=1, source_target_pairs={{0,24},{8,16},{16,8},{24,0},{1,25},{9,17},{17,9},{25,1},{2,26},{10... | collective-permute-start | bytes 307208 | tf_op jit(solution)/shard_map/ppermute | solution.py:399
  7.5 10.0 %collective-permute-start.1 = (bf16[2,200,128]{2,1,0:T(8,128)(2,1)S(1)}, bf16[2,200,128]{2,1,0:T(8,128)(2,1)S(1)}, u32[]{:S(2)}, u32[]{:S(2)}) collective-permute-start(bf16[2,200,128]{2,1,0:T(8,128)(2,1)S(1)} %pad_maximum_fusion.3), channel_id=1, source_target_pairs={{0,1},{1,0},{2,3},{3,2},{4,5},{5,4},{6,7},{7,6},{8,9},{9,8},{10,11... | collective-permute-start | bytes 307208 | tf_op jit(solution)/shard_map/ppermute | solution.py:399
  15.4 4.2 %collective-permute-start.3 = (bf16[1,200,128]{2,1,0:T(8,128)(2,1)S(1)}, bf16[1,200,128]{2,1,0:T(8,128)(2,1)S(1)}, u32[]{:S(2)}, u32[]{:S(2)}) collective-permute-start(bf16[1,200,128]{2,1,0:T(8,128)(2,1)S(1)} %get-tuple-element.34), channel_id=1, source_target_pairs={{0,1},{1,0},{2,3},{3,2},{4,5},{5,4},{6,7},{7,6},{8,9},{9,8},{10,11... | collective-permute-start | bytes 153608 | tf_op jit(solution)/shard_map/ppermute | solution.py:399
  16.9 4.2 %collective-permute-start.5 = (bf16[1,200,128]{2,1,0:T(8,128)(2,1)S(1)}, bf16[1,200,128]{2,1,0:T(8,128)(2,1)S(1)}, u32[]{:S(2)}, u32[]{:S(2)}) collective-permute-start(bf16[1,200,128]{2,1,0:T(8,128)(2,1)S(1)} %get-tuple-element.32), channel_id=1, source_target_pairs={{0,1},{1,0},{2,3},{3,2},{4,5},{5,4},{6,7},{7,6},{8,9},{9,8},{10,11... | collective-permute-start | bytes 153608 | tf_op jit(solution)/shard_map/ppermute | solution.py:399
  17.7 6.2 %collective-permute-start.6 = (bf16[4,200,128]{2,1,0:T(8,128)(2,1)S(1)}, bf16[4,200,128]{2,1,0:T(8,128)(2,1)S(1)}, u32[]{:S(2)}, u32[]{:S(2)}) collective-permute-start(bf16[4,200,128]{2,1,0:T(8,128)(2,1)S(1)} %pad_maximum_fusion.refs_0_), channel_id=1, source_target_pairs={{0,2},{2,0},{1,3},{3,1},{4,6},{6,4},{5,7},{7,5},{8,10},{10,8},{9,1... | collective-permute-start | bytes 614408 | tf_op jit(solution)/shard_map/ppermute | solution.py:399
  19.6 5.4 %collective-permute-start.7 = (bf16[2,200,128]{2,1,0:T(8,128)(2,1)S(1)}, bf16[2,200,128]{2,1,0:T(8,128)(2,1)S(1)}, u32[]{:S(2)}, u32[]{:S(2)}) collective-permute-start(bf16[2,200,128]{2,1,0:T(8,128)(2,1)S(1)} %pad_maximum_fusion.4.refs_1_), channel_id=1, source_target_pairs={{0,2},{2,0},{1,3},{3,1},{4,6},{6,4},{5,7},{7,5},{8,10},{10,8},{9,1... | collective-permute-start | bytes 307208 | tf_op jit(solution)/shard_map/ppermute | solution.py:399
  21.2 4.9 %collective-permute-start.8 = (bf16[2,200,128]{2,1,0:T(8,128)(2,1)S(1)}, bf16[2,200,128]{2,1,0:T(8,128)(2,1)S(1)}, u32[]{:S(2)}, u32[]{:S(2)}) collective-permute-start(bf16[2,200,128]{2,1,0:T(8,128)(2,1)S(1)} %pad_maximum_fusion.5.refs_2_), channel_id=1, source_target_pairs={{0,2},{2,0},{1,3},{3,1},{4,6},{6,4},{5,7},{7,5},{8,10},{10,8},{9,1... | collective-permute-start | bytes 307208 | tf_op jit(solution)/shard_map/ppermute | solution.py:399
  23.9 2.9 %collective-permute-start.9 = (bf16[8,200,128]{2,1,0:T(8,128)(2,1)S(1)}, bf16[8,200,128]{2,1,0:T(8,128)(2,1)S(1)}, u32[]{:S(2)}, u32[]{:S(2)}) collective-permute-start(bf16[8,200,128]{2,1,0:T(8,128)(2,1)S(1)} %constant_dynamic-update-slice_fusion), channel_id=1, source_target_pairs={{0,4},{4,0},{1,5},{5,1},{2,6},{6,2},{3,7},{7,3},{8,12},{12,8},{9,1... | collective-permute-start | bytes 1228808 | tf_op jit(solution)/shard_map/ppermute | solution.py:399
  25.0 2.4 %collective-permute-start.10 = (bf16[4,200,128]{2,1,0:T(8,128)(2,1)S(1)}, bf16[4,200,128]{2,1,0:T(8,128)(2,1)S(1)}, u32[]{:S(2)}, u32[]{:S(2)}) collective-permute-start(bf16[4,200,128]{2,1,0:T(8,128)(2,1)S(1)} %pad_maximum_fusion.1), channel_id=1, source_target_pairs={{0,4},{4,0},{1,5},{5,1},{2,6},{6,2},{3,7},{7,3},{8,12},{12,8},{9,1... | collective-permute-start | bytes 614408 | tf_op jit(solution)/shard_map/ppermute | solution.py:399
  26.1 1.5 %collective-permute-start.11 = (bf16[4,200,128]{2,1,0:T(8,128)(2,1)S(1)}, bf16[4,200,128]{2,1,0:T(8,128)(2,1)S(1)}, u32[]{:S(2)}, u32[]{:S(2)}) collective-permute-start(bf16[4,200,128]{2,1,0:T(8,128)(2,1)S(1)} %pad_maximum_fusion.2), channel_id=1, source_target_pairs={{0,4},{4,0},{1,5},{5,1},{2,6},{6,2},{3,7},{7,3},{8,12},{12,8},{9,1... | collective-permute-start | bytes 614408 | tf_op jit(solution)/shard_map/ppermute | solution.py:399
